TPU v7x, 512 devices: a whole 4x4x16 slice. The times are simulated.
512 devices in a mesh: vol: 32 (over z, core), view: 16 (over y, x).
Axes of the slice: x: 4, y: 4, z: 16, core: 2. Of those that a mesh axis runs over, the one named last changes fastest.
Arguments:
- volume: float32 [256, 1024], P('vol'), may hold values from -240 to 240
- footprint: int32 [32, 16, 32], P(None, 'view'), may hold values from 0 to 255, as said below
- offsets: int32 [32, 16, 32], P('vol', 'view'), may hold values from 0 to 1023
- ray_weights: bfloat16 [32, 16, 32, 4, 8192], P('vol', 'view'), may hold values from 0.049804688 to 1
- measured: float32 [32, 16, 8192], P('vol', 'view'), may hold values from -240 to 240
Outputs:
- correction: float32 [256, 1024], P('vol', 'view')
Inputs may be any that keep to these rules, and one draw needn't show every extreme that they name: Block b is owned by index b // 8 of vol. Each list footprint[o, g] names 32 distinct blocks: for some r and c, the blocks (r + i) * 8 + c + j for i < 16 and j < 2, in that order (i major).
All inputs are finite; a program needn't handle non-finite values.
Results may differ from a plain program's by a relative error of at most 0.0003.
Values sent between devices are 32-bit elements; how exact they have to be, the bound alone decides.
No kernel may reach another device: no remote copies, remote signals or barrier semaphores. Data moves between devices by JAX's collectives and lax.ppermute only.
A program may use at most 64 MiB of HBM per device.

v0:
```python
import jax
import jax.numpy as jnp
from jax import lax
from jax.sharding import PartitionSpec as P

VOXELS = 1024


def repeat_count(det_len, band_len, voxels):
    return (det_len + band_len + voxels - 1) // voxels


def rotate_rows(rows, firsts):
    voxels = rows.shape[-1]
    doubled = jnp.concatenate([rows, rows], axis=-1)
    return jax.vmap(
        lambda one_row, first: lax.dynamic_slice_in_dim(
            one_row, first, voxels, axis=one_row.ndim - 1
        )
    )(doubled, firsts)


def project(blocks, starts, ray_weights):
    band_len = ray_weights.shape[1]
    det_len = ray_weights.shape[2]
    foot_len = blocks.shape[0]
    voxels = blocks.shape[1]
    copies = repeat_count(det_len, band_len, voxels)
    rotated = rotate_rows(blocks, starts)
    windows = jnp.broadcast_to(rotated[:, None, :], (foot_len, copies, voxels)).reshape(
        foot_len, copies * voxels
    )
    total = jnp.zeros((det_len,), jnp.float32)
    for lag_index in range(band_len):
        total = total + jnp.sum(
            ray_weights[:, lag_index, :] * windows[:, lag_index : lag_index + det_len], axis=0
        )
    return total


def backproject(starts, ray_weights, residual_rays):
    band_len = ray_weights.shape[1]
    det_len = ray_weights.shape[2]
    foot_len = ray_weights.shape[0]
    voxels = VOXELS
    copies = repeat_count(det_len, band_len, voxels)
    length = copies * voxels
    cotangents = jnp.stack([residual_rays, jnp.ones_like(residual_rays)])
    spread = jnp.zeros((foot_len, 2, length), jnp.float32)
    for lag_index in range(band_len):
        products = ray_weights[:, None, lag_index, :] * cotangents[None, :, :]
        spread = spread + jnp.pad(
            products, ((0, 0), (0, 0), (lag_index, length - det_len - lag_index))
        )
    folded = jnp.sum(spread.reshape(foot_len, 2, copies, voxels), axis=2)
    return rotate_rows(folded, (voxels - starts) % voxels)


def shards(volume, footprint, offsets, ray_weights, measured):
    member = lax.axis_index("vol")
    blk_dev = volume.shape[0]
    block_lists = footprint[:, 0, :]
    own_list = lax.dynamic_index_in_dim(block_lists, member, 0, keepdims=False)
    gathered = lax.all_gather(volume, "vol", axis=0, tiled=True)
    blocks = jnp.take(gathered, own_list, axis=0)
    starts = offsets[0, 0]
    weight_set = ray_weights[0, 0]
    projection = project(blocks, starts, weight_set)
    row_sum = jnp.sum(weight_set, axis=(0, 1), dtype=jnp.float32)
    residual_rays = (measured[0, 0] - projection) / row_sum
    partials = backproject(starts, weight_set, residual_rays)
    targets = jnp.arange(blk_dev * lax.axis_size("vol"))
    selector = (own_list[None, :] == targets[:, None]).astype(jnp.float32)
    summed = lax.psum_scatter(
        jnp.einsum("bf,fcv->bcv", selector, partials, precision=lax.Precision.HIGHEST),
        "vol",
        scatter_dimension=0,
        tiled=True,
    )
    totals = lax.psum_scatter(summed, "view", scatter_dimension=2, tiled=True)
    return totals[:, 0] / jnp.maximum(totals[:, 1], 1.0)


def solution(mesh):
    in_specs = (
        P("vol", None),
        P(None, "view", None),
        P("vol", "view", None),
        P("vol", "view", None, None, None),
        P("vol", "view", None),
    )
    out_specs = P("vol", "view")
    return jax.shard_map(shards, mesh=mesh, in_specs=in_specs, out_specs=out_specs, check_vma=False)
```

profile of v0, /device:TPU:1, one launch (start us, length us, event | category | flops | bytes accessed | tf_op | source)
XLA Modules:
  0.0 480.9 jit_solution(8750689981459907678)
XLA Ops:
  8.0 2.7 convert_reduce_fusion
  12.1 2.7 copy.36
  14.9 1.7 fusion.7
  16.6 69.3 %all-gather.2.cloned.1.call-done = f32[256,1024]{1,0:T(8,128)} async-done(((f32[8,1024]{1,0:T(8,128)}), f32[256,1024]{1,0:T(8,128)}) %all-gather.2.cloned.1.call-update) | async-done | bytes 1048592 | tf_op jit(solution)/shard_map/all_gather | solution.py:64
  85.9 1.9 gather_fusion
  87.9 110.4 %while.2 = (s32[]{:T(128)}, f32[32,2048]{1,0:T(8,128)S(1)}, s32[32,2]{0,1:T(2,128)S(1)}, f32[32,1024]{1,0:T(8,128)}, s32[]{:T(128)}, /*index=5*/s32[]{:T(128)}) while((s32[]{:T(128)}, f32[32,2048]{1,0:T(8,128)S(1)}, s32[32,2]{0,1:T(2,128)S(1)}, f32[32,1024]{1,0:T(8,128)}, s32[]{:T(128)}, /*index=5*/s32[]{:T(128)}) %tuple.46), condition=%wide.while_cond, body=%wide.while_body.sunk | while | flops 2 | bytes 16497 | solution.py:17
  88.6 1.4 dynamic-slice.16
  95.5 1.4 dynamic-slice.16
  98.9 1.4 dynamic-slice.16
  117.5 1.4 dynamic-update-slice.6
  121.0 1.4 dynamic-update-slice.6
  124.4 1.4 dynamic-update-slice.6
  127.9 1.4 dynamic-update-slice.6
  131.3 1.4 dynamic-update-slice.6
  134.8 1.4 dynamic-update-slice.6
  138.3 1.4 dynamic-update-slice.6
  141.7 1.4 dynamic-update-slice.6
  172.8 1.4 dynamic-update-slice.6
  176.2 1.4 dynamic-update-slice.6
  179.7 1.4 dynamic-update-slice.6
  183.1 1.4 dynamic-update-slice.6
  186.6 1.4 dynamic-update-slice.6
  190.0 1.4 dynamic-update-slice.6
  193.5 1.4 dynamic-update-slice.6
  196.9 1.4 dynamic-update-slice.6
  203.0 1.7 pad_add_fusion
  204.7 2.2 reshape.182
  206.9 3.2 reduce_sum.62
  210.2 64.7 %while.3 = (s32[]{:T(128)}, f32[32,2,2048]{2,0,1:T(8,128)S(1)}, s32[32,3]{0,1:T(4,128)S(1)}, f32[32,2,1024]{2,0,1:T(8,128)S(1)}, s32[]{:T(128)}, /*index=5*/s32[]{:T(128)}) while((s32[]{:T(128)}, f32[32,2,2048]{2,0,1:T(8,128)S(1)}, s32[32,3]{0,1:T(4,128)S(1)}, f32[32,2,1024]{2,0,1:T(8,128)S(1)}, s32[]{:T(128)}, /*index=5*/s32[]{:T(128)}) %tuple.58), condition=%wide.while_cond.1, body=%wide.while_body.1.sunk | while | flops 2 | bytes 32893 | solution.py:17
  274.9 2.4 fusion.10
  277.4 103.9 %reduce-scatter.5.cloned.1.call-done = f32[8,2,1024]{2,0,1:T(8,128)} async-done(((f32[256,2,1024]{2,0,1:T(8,128)}), f32[8,2,1024]{2,0,1:T(8,128)}) %reduce-scatter.5.cloned.1.call-update) | async-done | bytes 65552 | tf_op jit(solution)/shard_map/reduce_scatter | solution.py:74
  384.0 88.7 %reduce-scatter.7.cloned.1.call-done = f32[64,16]{1,0:T(8,128)} async-done(((f32[1024,16]{1,0:T(8,128)}), f32[64,16]{1,0:T(8,128)}) %reduce-scatter.7.cloned.1.call-update) | async-done | bytes 4112
  (280 shorter events, 159.7 us)
Async XLA Ops:
  6.5 79.3 %all-gather.2.cloned.1.call-start = ((), (), s32[]{:S(2)}) async-start(), calls=%async_computation.2 | async-start | bytes 1081344 | tf_op jit(solution)/shard_map/all_gather | solution.py:64
  7.3 374.1 %reduce-scatter.5.cloned.1.call-start = ((), (), s32[]{:S(2)}) async-start(), calls=%async_computation.3 | async-start | bytes 2162688 | tf_op jit(solution)/shard_map/reduce_scatter | solution.py:74
  200.2 1.1 copy-start.4
  200.2 1.2 copy-start
  200.2 1.5 copy-start.1
  200.2 1.8 copy-start.2
  206.9 3.2 copy-start.3
  277.3 195.4 %reduce-scatter.7.cloned.1.call-start = ((), (), s32[]{:S(2)}) async-start(), calls=%async_computation.4 | async-start | bytes 557056
Sparse Core Ops, SparseCore 0:
  9.5 76.3 all-gather.1
  277.4 103.8 reduce-scatter.4
  385.9 86.7 reduce-scatter.6
where the time goes:
time: 485 us; the launch traced here: 481 us
  waiting for transfers between devices  263 us (54%)
  local copies, waits for them, and re-layouts  187 us (39%)
  other arithmetic  14.2 us (3%)
  between operations  13.3 us (3%)
    gather x256, local copies, waits for them, and re-layouts  174 us
    reduce_scatter x1, waiting for transfers between devices, shards(): lax.psum_scatter(jnp.einsum('bf,fcv->bcv', selector, partials, precision=...  104 us
    unnamed x4, waiting for transfers between devices  89.4 us
    all_gather x1, waiting for transfers between devices, shards(): gathered = lax.all_gather(volume, 'vol', axis=0, tiled=True)  69.3 us
  transfers between devices with their start and end apart: 3, of which 3 were waited for; matrix products, arithmetic and copies ran while one was open for 2% of the time, Pallas kernels for 0%

commit v1 on v0

v1 whole, which is shorter than its diff:
```python
import functools

import jax
import jax.numpy as jnp
from jax import lax
from jax.experimental import pallas as pl
from jax.experimental.pallas import tpu as pltpu
from jax.sharding import PartitionSpec as P

VOXELS = 1024
LANES = 128
TILES = VOXELS // LANES
FOOT = 32
BAND = 4
FOLDS = 8
BLK = 8
N_Z = 16
N_VIEW = 16
MSG = FOOT + 8
SUB = VOXELS // N_VIEW

VMEM = pl.BlockSpec(memory_space=pltpu.VMEM)
SMEM = pl.BlockSpec(memory_space=pltpu.SMEM)
F32 = jnp.float32
BF16 = jnp.bfloat16


def rotate_left(rows, amount):
    amount %= VOXELS
    return rows if amount == 0 else pltpu.roll(rows, VOXELS - amount, 1)


def rotate_right(rows, amount):
    return rotate_left(rows, VOXELS - amount)


def rotate_each(rows, counts, rotate):
    wide = jnp.concatenate([counts] * TILES, axis=1)
    for bit in range(10):
        rows = jnp.where((wide >> bit) & 1 == 1, rotate(rows, 1 << bit), rows)
    return rows


def split3(x):
    high = x.astype(BF16)
    rest = x - high.astype(F32)
    mid = rest.astype(BF16)
    low = (rest - mid.astype(F32)).astype(BF16)
    return high, mid, low


def fold_lags(spread_ref, counts):
    total = spread_ref[BAND - 1]
    for lag in range(BAND - 2, -1, -1):
        total = rotate_right(total, 1) + spread_ref[lag]
    return rotate_each(total, counts, rotate_right)


def weight_tile(weights_ref, lag, fold, tile):
    first = pl.multiple_of(fold * VOXELS + tile * LANES, LANES)
    return weights_ref[lag, :, pl.ds(first, LANES)].astype(F32)


def sum_rows(tile):
    part = tile[0:8] + tile[8:16] + tile[16:24] + tile[24:32]
    return jnp.sum(part, axis=0, keepdims=True)


def pick_kernel(core_ref, foot_ref, own_ref, other_ref, out_ref, rows_ref):
    core = core_ref[0]
    for side, ref in enumerate((own_ref, other_ref)):
        for tile in range(TILES):
            rows_ref[pl.ds(side * BLK * TILES + tile, BLK, stride=TILES), :] = ref[:, tile * LANES : (tile + 1) * LANES]
    for z in range(N_Z):
        column = foot_ref[2 * z + core, 0] & (BLK - 1)
        for side in range(2):
            first = pl.multiple_of((side * BLK + column) * TILES, TILES)
            out_ref[z, side * 2 * TILES : (side + 1) * 2 * TILES, :] = rows_ref[pl.ds(first, 2 * TILES), :]


def sums_kernel(weights_ref, counts_ref, column_ref, row_ref, spread_ref):
    def tile_step(tile, carry):
        lanes = pl.ds(pl.multiple_of(tile * LANES, LANES), LANES)
        spread = [jnp.zeros((FOOT, LANES), F32) for _ in range(BAND)]
        rows = []
        for fold in range(FOLDS):
            total = jnp.zeros((FOOT, LANES), F32)
            for lag in range(BAND):
                weights = weight_tile(weights_ref, lag, fold, tile)
                spread[lag] = spread[lag] + weights
                total = total + weights
            rows.append(sum_rows(total))
        row_ref[:, lanes] = jnp.concatenate(rows, axis=0)
        for lag in range(BAND):
            spread_ref[lag, :, lanes] = spread[lag]
        return carry

    lax.fori_loop(0, TILES, tile_step, 0)
    column_ref[...] = fold_lags(spread_ref, counts_ref[...])


def rays_kernel(
    place_ref, blocks_ref, weights_ref, counts_ref, measured_ref, row_ref, column_ref, out_ref, window_ref, spread_ref
):
    core, first_block = place_ref[0], place_ref[1]
    first_owner = first_block >> 3
    shape = (FOOT, 2 * FOOT)
    foot = lax.broadcasted_iota(jnp.int32, shape, 0)
    slot = lax.broadcasted_iota(jnp.int32, shape, 1)
    owner = first_owner + (foot >> 1)
    side = (owner & 1) ^ core
    wanted = (side * 2 + (foot & 1)) * N_Z + (owner >> 1)
    chosen = (slot == wanted).astype(F32).astype(BF16)
    chosen = jnp.concatenate([chosen] * 3, axis=1)
    pieces = []
    for tile in range(TILES):
        rows = [blocks_ref[pl.ds(line * TILES + tile, N_Z, stride=4 * TILES), :] for line in range(4)]
        pieces.append(jnp.concatenate(rows, axis=0))
    sent = jnp.concatenate(pieces, axis=1)
    covered = jnp.dot(chosen, jnp.concatenate(split3(sent), axis=0), preferred_element_type=F32)
    counts = counts_ref[...]
    window = rotate_each(covered, counts, rotate_left)
    window_ref[0] = window
    for lag in range(1, BAND):
        window_ref[lag] = rotate_left(window, lag)

    def tile_step(tile, carry):
        lanes = pl.ds(pl.multiple_of(tile * LANES, LANES), LANES)
        rows = []
        windows = [window_ref[lag, :, lanes] for lag in range(BAND)]
        for fold in range(FOLDS):
            total = weight_tile(weights_ref, 0, fold, tile) * windows[0]
            for lag in range(1, BAND):
                total = total + weight_tile(weights_ref, lag, fold, tile) * windows[lag]
            rows.append(sum_rows(total))
        projection = jnp.concatenate(rows, axis=0)
        residual = (measured_ref[:, lanes] - projection) / row_ref[:, lanes]
        for lag in range(BAND):
            spread = weight_tile(weights_ref, lag, 0, tile) * residual[0:1]
            for fold in range(1, FOLDS):
                spread = spread + weight_tile(weights_ref, lag, fold, tile) * residual[fold : fold + 1]
            spread_ref[lag, :, lanes] = spread
        return carry

    lax.fori_loop(0, TILES, tile_step, 0)
    back = fold_lags(spread_ref, counts)
    low = lax.broadcasted_iota(jnp.int32, (FOOT, LANES), 1) < SUB
    base = jnp.full((8, LANES), first_block, jnp.int32).astype(F32)
    for tile in range(TILES):
        sums = back[:, tile * LANES : (tile + 1) * LANES]
        columns = column_ref[:, tile * LANES : (tile + 1) * LANES]
        out_ref[2 * tile, 0:FOOT, :] = jnp.where(low, sums, pltpu.roll(columns, SUB, 1))
        out_ref[2 * tile + 1, 0:FOOT, :] = jnp.where(low, pltpu.roll(sums, SUB, 1), columns)
        out_ref[2 * tile, FOOT:MSG, :] = base
        out_ref[2 * tile + 1, FOOT:MSG, :] = base


def place_kernel(parts_ref, out_ref):
    lane = lax.broadcasted_iota(jnp.int32, (1, LANES), 1)
    within = (((lane & (FOOT - 1)) >> 1) * BLK + (lane & 1)).astype(F32)
    quarter = lane >> 5
    targets = []
    for group in range(0, N_VIEW, 4):
        first = parts_ref[group, FOOT : FOOT + 1, :]
        for other in range(1, 4):
            first = jnp.where(quarter == other, parts_ref[group + other, FOOT : FOOT + 1, :], first)
        targets.append(first + within)
    target = jnp.concatenate(targets, axis=1)
    block = lax.broadcasted_iota(jnp.int32, (2 * FOLDS * N_Z, N_VIEW * FOOT), 0).astype(F32)
    chosen = jnp.where(block == target, 1.0, 0.0).astype(BF16)
    parts = jnp.concatenate([parts_ref[group, 0:FOOT, :] for group in range(N_VIEW)], axis=0)
    high, mid, low = split3(parts)
    both = jnp.dot(chosen, jnp.concatenate([high, mid], axis=1), preferred_element_type=F32)
    total = both[:, :LANES] + (both[:, LANES:] + jnp.dot(chosen, low, preferred_element_type=F32))
    out_ref[...] = total


def finish_kernel(mine_ref, theirs_ref, out_ref):
    total = mine_ref[...] + theirs_ref[...]
    columns = pltpu.roll(total, SUB, 1)
    out_ref[...] = (total / jnp.maximum(columns, 1.0))[:, :SUB]


def call(kernel, out_shape, in_specs, scratch=(), cost=None):
    return pl.pallas_call(
        kernel,
        out_shape=out_shape,
        in_specs=in_specs,
        out_specs=jax.tree.map(lambda _: VMEM, out_shape),
        scratch_shapes=scratch,
        cost_estimate=cost,
        compiler_params=pltpu.CompilerParams(vmem_limit_bytes=24 * 2**20),
    )


def shards(volume, footprint, offsets, ray_weights, measured):
    member = lax.axis_index("vol")
    core = member & 1
    swap = [(i, i ^ 1) for i in range(2 * N_Z)]
    chips = [[2 * z + c for z in range(N_Z)] for c in range(2)]
    lists = footprint[:, 0, :]

    other = lax.ppermute(volume, "vol", swap)
    sent = call(
        pick_kernel,
        jax.ShapeDtypeStruct((N_Z, 4 * TILES, LANES), F32),
        [SMEM, SMEM, VMEM, VMEM],
        [pltpu.VMEM((2 * BLK * TILES, LANES), F32)],
    )(core[None], lists, volume, other)
    blocks = lax.all_to_all(sent, "vol", 0, 0, axis_index_groups=chips)

    weights = jnp.transpose(ray_weights[0, 0], (1, 0, 2))
    counts = jnp.broadcast_to(offsets[0, 0][:, None], (FOOT, LANES))
    work = BAND * FOOT * FOLDS * VOXELS
    columns, row_sum = call(
        sums_kernel,
        (jax.ShapeDtypeStruct((FOOT, VOXELS), F32), jax.ShapeDtypeStruct((FOLDS, VOXELS), F32)),
        [VMEM, VMEM],
        [pltpu.VMEM((BAND, FOOT, VOXELS), F32)],
        pl.CostEstimate(flops=2 * work, bytes_accessed=2 * work, transcendentals=0),
    )(weights, counts)

    first_block = lax.dynamic_index_in_dim(lists, member, 0, keepdims=False)[0]
    parts = call(
        rays_kernel,
        jax.ShapeDtypeStruct((N_VIEW, MSG, LANES), F32),
        [SMEM] + [VMEM] * 6,
        [pltpu.VMEM((BAND, FOOT, VOXELS), F32), pltpu.VMEM((BAND, FOOT, VOXELS), F32)],
        pl.CostEstimate(flops=4 * work, bytes_accessed=2 * work, transcendentals=0),
    )(
        jnp.stack([core, first_block]),
        blocks.reshape(N_Z * 4 * TILES, LANES),
        weights,
        counts,
        measured.reshape(FOLDS, VOXELS),
        row_sum,
        columns,
    )
    parts = lax.all_to_all(parts, "view", 0, 0)
    placed = call(place_kernel, jax.ShapeDtypeStruct((N_Z * 2 * BLK, LANES), F32), [VMEM])(parts)
    placed = lax.all_to_all(placed.reshape(N_Z, 2, BLK, LANES), "vol", 0, 0, axis_index_groups=chips)
    summed = jnp.sum(placed, axis=0)
    mine = lax.dynamic_index_in_dim(summed, core, 0, keepdims=False)
    theirs = lax.ppermute(lax.dynamic_index_in_dim(summed, 1 - core, 0, keepdims=False), "vol", swap)
    return call(finish_kernel, jax.ShapeDtypeStruct((BLK, SUB), F32), [VMEM, VMEM])(mine, theirs)


def solution(mesh):
    in_specs = (
        P("vol", None),
        P(None, "view", None),
        P("vol", "view", None),
        P("vol", "view", None, None, None),
        P("vol", "view", None),
    )
    return jax.shard_map(shards, mesh=mesh, in_specs=in_specs, out_specs=P("vol", "view"), check_vma=False)
```

time: 485 us -> 86.6 us (0.18)
  waiting for transfers between devices: 263 us -> 21.1 us
  local copies, waits for them, and re-layouts: 187 us -> 5.54 us
  starting transfers between devices: 0.08 us -> 35.1 us
  blocking collectives: 0 us -> 14.4 us
  other arithmetic: 14.2 us -> 0.83 us
  between operations: 13.3 us -> 0.12 us
  Pallas kernels: 0 us -> 8.96 us
    gather x257 -> x0, local copies, waits for them, and re-layouts: 176 us -> none
    reduce_scatter x1 -> x0, waiting for transfers between devices: 104 us -> none  [shards(): lax.psum_scatter(jnp.einsum('bf,fcv->bcv', selector, partials, precision=...]
    unnamed x4 -> x0, waiting for transfers between devices: 89.4 us -> none
    all_gather x1 -> x0, waiting for transfers between devices: 69.3 us -> none  [shards(): gathered = lax.all_gather(volume, 'vol', axis=0, tiled=True)]
    all_to_all x0 -> x2, starting transfers between devices: none -> 20.4 us  [the longest x1 10.8 us: shards(): lax.all_to_all(placed.reshape(N_Z, 2, BLK, LANES), 'vol', 0, 0, axis_inde...]
    all_to_all x0 -> x2, waiting for transfers between devices: none -> 19.2 us  [the longest x1 12 us: shards(): lax.all_to_all(placed.reshape(N_Z, 2, BLK, LANES), 'vol', 0, 0, axis_inde...]
    ppermute x0 -> x2, starting transfers between devices: none -> 14.7 us  [the longest x1 8.77 us: shards(): other = lax.ppermute(volume, 'vol', swap)]
    all_to_all x0 -> x1, blocking collectives: none -> 14.4 us  [shards(): parts = lax.all_to_all(parts, 'view', 0, 0)]
  transfers between devices with their start and end apart: 3 -> 4, of which waited for: 3 -> 4; matrix products, arithmetic and copies ran while one was open for 2% -> 6% of each run, Pallas kernels for 0% -> 2%
where the time goes in v1:
time: 86.6 us; the launch traced here: 86.1 us
  starting transfers between devices  35.1 us (41%)
  waiting for transfers between devices  21.1 us (24%)
  blocking collectives  14.4 us (17%)
  Pallas kernels  8.96 us (10%)
  local copies, waits for them, and re-layouts  5.54 us (6%)
    all_to_all x1, blocking collectives, shards(): parts = lax.all_to_all(parts, 'view', 0, 0)  14.4 us
    all_to_all x1, waiting for transfers between devices, shards(): lax.all_to_all(placed.reshape(N_Z, 2, BLK, LANES), 'vol', 0, 0, axis_inde...  12 us
    all_to_all x1, starting transfers between devices, shards(): lax.all_to_all(placed.reshape(N_Z, 2, BLK, LANES), 'vol', 0, 0, axis_inde...  10.8 us
    all_to_all x1, starting transfers between devices, shards(): blocks = lax.all_to_all(sent, 'vol', 0, 0, axis_index_groups=chips)  9.54 us
    ppermute x1, starting transfers between devices, shards(): other = lax.ppermute(volume, 'vol', swap)  8.77 us
    all_to_all x1, waiting for transfers between devices, shards(): blocks = lax.all_to_all(sent, 'vol', 0, 0, axis_index_groups=chips)  7.24 us
    ppermute x1, starting transfers between devices, shards(): lax.ppermute(lax.dynamic_index_in_dim(summed, 1 - core, 0, keepdims=False...  5.92 us
    unnamed x10, local copies, waits for them, and re-layouts  4.79 us
  transfers between devices with their start and end apart: 4, of which 4 were waited for; matrix products, arithmetic and copies ran while one was open for 6% of the time, Pallas kernels for 2%

profile of v1, /device:TPU:1, one launch (start us, length us, event | category | flops | bytes accessed | tf_op | source)
XLA Modules:
  0.0 86.1 jit_solution(5230505959982153199)
XLA Ops:
  0.0 8.8 %collective-permute-start = (f32[8,1024]{1,0:T(8,128)}, f32[8,1024]{1,0:T(8,128)S(1)}, u32[]{:S(2)}, u32[]{:S(2)}) collective-permute-start(f32[8,1024]{1,0:T(8,128)} %own_ref.1), channel_id=1, source_target_pairs={{0,16},{16,0},{32,48},{48,32},{64,80},{80,64},{96,112},{112,96},{1... | collective-permute-start | bytes 98312 | tf_op jit(solution)/shard_map/ppermute | solution.py:203
  8.8 1.0 %collective-permute-done.other_ref = f32[8,1024]{1,0:T(8,128)S(1)} collective-permute-done((f32[8,1024]{1,0:T(8,128)}, f32[8,1024]{1,0:T(8,128)S(1)}, u32[]{:S(2)}, u32[]{:S(2)}) %collective-permute-start) | collective-permute-done | bytes 32800 | tf_op jit(solution)/shard_map/ppermute | solution.py:203
  9.8 0.0 copy-start
  9.8 0.8 copy-done
  10.6 0.0 copy-start.1
  10.6 0.7 copy-done.1
  11.3 1.5 %shard_map.55 = f32[16,32,128]{2,1,0:T(8,128)} custom-call(s32[1]{0:T(128)} %bitcast.core_ref, s32[32,32]{1,0:T(8,128)S(1)} %bitcast.19, f32[8,1024]{1,0:T(8,128)S(1)} %copy-done, f32[8,1024]{1,0:T(8,128)S(1)} %collective-permute-done.other_ref), custom_call_target="tpu_custom_call" | custom-call | tf_op jit(solution)/shard_map/pallas_call | solution.py:204
  12.8 9.5 %all-to-all-start = ((f32[16,32,128]{2,1,0:T(8,128)}), f32[16,32,128]{2,1,0:T(8,128)S(1)}, u32[]{:S(2)}, u32[]{:S(2)}) async-start(f32[16,32,128]{2,1,0:T(8,128)} %shard_map.55), calls=%async_computation | async-start | bytes 524288 | tf_op jit(solution)/shard_map/all_to_all | solution.py:210
  22.4 0.0 copy-start.2
  22.4 0.0 copy-start.3
  22.4 2.8 %copy.8 = bf16[1,1,32,4,8192]{4,2,3,1,0:T(8,128)(2,1)S(1)} copy(bf16[1,1,32,4,8192]{4,3,2,1,0:T(4,128)(2,1)} %param.8) | data formatting | bytes 4194304 | tf_op args[3]
  25.2 0.5 broadcast.3
  25.7 0.0 copy-done.2
  25.7 0.7 reduce.3
  26.5 0.0 copy-done.3
  26.5 0.1 broadcast_in_dim.9.counts_ref
  26.5 1.9 %shard_map.56 = (f32[32,1024]{1,0:T(8,128)S(1)}, f32[8,1024]{1,0:T(8,128)S(1)}) custom-call(bf16[4,32,8192]{2,1,0:T(8,128)(2,1)S(1)} %bitcast.16, s32[32,128]{1,0:T(8,128)S(1)} %broadcast_in_dim.9.counts_ref), custom_call_target="tpu_custom_call" | custom-call | flops 2097152 | bytes 2097152 | tf_op jit(solution)/shard_map/pallas_call | solution.py:215
  28.4 0.7 constant_dynamic-slice_fusion
  29.1 0.1 pad_add_fusion.place_ref
  29.2 7.2 %all-to-all-done = f32[16,32,128]{2,1,0:T(8,128)S(1)} async-done(((f32[16,32,128]{2,1,0:T(8,128)}), f32[16,32,128]{2,1,0:T(8,128)S(1)}, u32[]{:S(2)}, u32[]{:S(2)}) %all-to-all-start) | async-done | bytes 262176 | tf_op jit(solution)/shard_map/all_to_all | solution.py:210
  36.4 3.9 %shard_map.57 = f32[16,40,128]{2,1,0:T(8,128)S(1)} custom-call(s32[2]{0:T(128)S(1)} %pad_add_fusion.place_ref, f32[512,128]{1,0:T(8,128)S(1)} %bitcast.18, bf16[4,32,8192]{2,1,0:T(8,128)(2,1)S(1)} %bitcast.17, s32[32,128]{1,0:T(8,128)S(1)} %broadcast_in_dim.9.counts_ref, f32[8,1024]{1,0:T(8,128)S(1)} %reshape.14.measured_ref, ...), custom_call_target="tpu_custom_call" | custom-call | flops 4194304 | bytes 2097152 | tf_op jit(solution)/shard_map/pallas_call | solution.py:224
  40.4 14.4 %all_to_all.15.parts_ref = f32[16,40,128]{2,1,0:T(8,128)S(1)} all-to-all(f32[16,40,128]{2,1,0:T(8,128)S(1)} %shard_map.57), channel_id=1, replica_groups=mesh['vol'=32,'view'=16] {'view'}, dimensions={0} | all-to-all | bytes 655360 | tf_op jit(solution)/shard_map/all_to_all | solution.py:239
  54.8 1.0 %shard_map.58 = f32[256,128]{1,0:T(8,128)} custom-call(f32[16,40,128]{2,1,0:T(8,128)S(1)} %all_to_all.15.parts_ref), custom_call_target="tpu_custom_call" | custom-call | tf_op jit(solution)/shard_map/pallas_call | solution.py:240
  55.8 10.8 %all-to-all-start.2 = ((f32[16,2,8,128]{3,2,1,0:T(8,128)}), f32[16,2,8,128]{3,2,1,0:T(8,128)S(1)}, u32[]{:S(2)}, u32[]{:S(2)}) async-start(f32[16,2,8,128]{3,2,1,0:T(8,128)} %bitcast.8), calls=%async_computation.2 | async-start | bytes 262144 | tf_op jit(solution)/shard_map/all_to_all | solution.py:241
  66.6 12.0 %all-to-all-done.2 = f32[16,2,8,128]{3,2,1,0:T(8,128)S(1)} async-done(((f32[16,2,8,128]{3,2,1,0:T(8,128)}), f32[16,2,8,128]{3,2,1,0:T(8,128)S(1)}, u32[]{:S(2)}, u32[]{:S(2)}) %all-to-all-start.2) | async-done | bytes 131104 | tf_op jit(solution)/shard_map/all_to_all | solution.py:241
  78.6 5.9 %collective-permute-start.1 = (f32[8,128]{1,0:T(8,128)S(1)}, f32[8,128]{1,0:T(8,128)S(1)}, u32[]{:S(2)}, u32[]{:S(2)}) collective-permute-start(f32[8,128]{1,0:T(8,128)S(1)} %get-tuple-element.9), channel_id=1, source_target_pairs={{0,16},{16,0},{32,48},{48,32},{64,80},{80,64},{96,112},{112,96},{1... | collective-permute-start | bytes 12296 | tf_op jit(solution)/shard_map/ppermute | solution.py:244
  84.6 0.8 collective-permute-done.1.theirs_ref
  85.4 0.7 shard_map.59
  (3 shorter events, 0.0 us)
Async XLA Ops:
  0.0 9.8 %collective-permute-start = (f32[8,1024]{1,0:T(8,128)}, f32[8,1024]{1,0:T(8,128)S(1)}, u32[]{:S(2)}, u32[]{:S(2)}) collective-permute-start(f32[8,1024]{1,0:T(8,128)} %own_ref.1), channel_id=1, source_target_pairs={{0,16},{16,0},{32,48},{48,32},{64,80},{80,64},{96,112},{112,96},{1... | collective-permute-start | bytes 98312 | tf_op jit(solution)/shard_map/ppermute | solution.py:203
  9.8 0.8 copy-start
  10.6 0.7 copy-start.1
  12.8 23.6 %all-to-all-start = ((f32[16,32,128]{2,1,0:T(8,128)}), f32[16,32,128]{2,1,0:T(8,128)S(1)}, u32[]{:S(2)}, u32[]{:S(2)}) async-start(f32[16,32,128]{2,1,0:T(8,128)} %shard_map.55), calls=%async_computation | async-start | bytes 524288 | tf_op jit(solution)/shard_map/all_to_all | solution.py:210
  22.4 3.3 %copy-start.2 = (f32[1,1,8192]{2,1,0:T(1,128)S(1)}, f32[1,1,8192]{2,1,0:T(1,128)}, u32[]{:S(2)}) copy-start(f32[1,1,8192]{2,1,0:T(1,128)} %param.9) | copy-start | bytes 98308
  22.4 4.1 %copy-start.3 = (s32[1,1,32]{2,1,0:T(1,128)S(1)}, s32[1,1,32]{2,1,0:T(1,128)}, u32[]{:S(2)}) copy-start(s32[1,1,32]{2,1,0:T(1,128)} %param.7) | copy-start | bytes 388
  55.8 22.8 %all-to-all-start.2 = ((f32[16,2,8,128]{3,2,1,0:T(8,128)}), f32[16,2,8,128]{3,2,1,0:T(8,128)S(1)}, u32[]{:S(2)}, u32[]{:S(2)}) async-start(f32[16,2,8,128]{3,2,1,0:T(8,128)} %bitcast.8), calls=%async_computation.2 | async-start | bytes 262144 | tf_op jit(solution)/shard_map/all_to_all | solution.py:241
  78.6 6.7 %collective-permute-start.1 = (f32[8,128]{1,0:T(8,128)S(1)}, f32[8,128]{1,0:T(8,128)S(1)}, u32[]{:S(2)}, u32[]{:S(2)}) collective-permute-start(f32[8,128]{1,0:T(8,128)S(1)} %get-tuple-element.9), channel_id=1, source_target_pairs={{0,16},{16,0},{32,48},{48,32},{64,80},{80,64},{96,112},{112,96},{1... | collective-permute-start | bytes 12296 | tf_op jit(solution)/shard_map/ppermute | solution.py:244

commit v2 on v1

v2 whole, which is shorter than its diff:
```python
import jax
import jax.numpy as jnp
from jax import lax
from jax.experimental import pallas as pl
from jax.experimental.pallas import tpu as pltpu
from jax.sharding import PartitionSpec as P

VOXELS = 1024
LANES = 128
TILES = VOXELS // LANES
FOOT = 32
HALF = FOOT // 2
BAND = 4
FOLDS = 8
BLK = 8
N_Z = 16
N_VIEW = 16
PEERS = 2 * N_VIEW
MSG = HALF + 8
SUB = VOXELS // N_VIEW

VMEM = pl.BlockSpec(memory_space=pltpu.VMEM)
SMEM = pl.BlockSpec(memory_space=pltpu.SMEM)
ANY = pl.BlockSpec(memory_space=pl.ANY)
F32 = jnp.float32
BF16 = jnp.bfloat16


def lane_tiles(rows):
    return [rows[:, tile * LANES : (tile + 1) * LANES] for tile in range(TILES)]


def rotate_each(tiles, counts, left):
    lane = lax.broadcasted_iota(jnp.int32, (FOOT, LANES), 1)
    within = counts & (LANES - 1)
    source = (lane + within if left else lane - within) & (LANES - 1)
    same = lane + within < LANES if left else lane >= within
    step = 1 if left else TILES - 1
    moved = [jnp.take_along_axis(tile, source, axis=1) for tile in tiles]
    tiles = [jnp.where(same, moved[t], moved[(t + step) % TILES]) for t in range(TILES)]
    for bit in range(3):
        far = step << bit
        chosen = (counts >> (7 + bit)) & 1 == 1
        tiles = [jnp.where(chosen, tiles[(t + far) % TILES], tiles[t]) for t in range(TILES)]
    return tiles


def split3(x):
    high = x.astype(BF16)
    rest = x - high.astype(F32)
    mid = rest.astype(BF16)
    low = (rest - mid.astype(F32)).astype(BF16)
    return high, mid, low


def fold_lags(spread_ref, counts):
    total = spread_ref[BAND - 1]
    for lag in range(BAND - 2, -1, -1):
        total = pltpu.roll(total, 1, 1) + spread_ref[lag]
    return rotate_each(lane_tiles(total), counts, False)


def sum_rows(totals):
    row = lax.broadcasted_iota(jnp.int32, (8, LANES), 0)
    low = row < 4
    fours = [
        jnp.where(low, totals[k], totals[k + 4]) + pltpu.roll(jnp.where(low, totals[k + 4], totals[k]), 4, 0)
        for k in range(4)
    ]

    def halve(parts, width):
        first = row & width == 0
        count = len(parts) // 2
        return [
            jnp.where(
                first,
                parts[k] + pltpu.roll(parts[k], 8 - width, 0),
                parts[k + count] + pltpu.roll(parts[k + count], width, 0),
            )
            for k in range(count)
        ]

    return halve(halve(fours, 2), 1)[0]


def quarter(tile):
    return tile[0:8] + tile[8:16] + tile[16:24] + tile[24:32]


def lanes_of(fold, tile):
    return pl.ds(pl.multiple_of(fold * VOXELS + tile * LANES, LANES), LANES)


def pick_kernel(core_ref, foot_hbm, own_hbm, other_ref, out_ref, rows_ref, own_ref, foot_ref, sems):
    foot_copy = pltpu.make_async_copy(foot_hbm, foot_ref, sems.at[0])
    own_copy = pltpu.make_async_copy(own_hbm, own_ref, sems.at[1])
    foot_copy.start()
    own_copy.start()
    core = core_ref[0]

    def spread_rows(side, ref):
        for tile in range(TILES):
            rows_ref[pl.ds(side * BLK * TILES + tile, BLK, stride=TILES), :] = ref[:, tile * LANES : (tile + 1) * LANES]

    spread_rows(1, other_ref)
    own_copy.wait()
    spread_rows(0, own_ref)
    foot_copy.wait()
    for z in range(N_Z):
        column = foot_ref[2 * z + core, 0, 0] & (BLK - 1)
        for side in range(2):
            first = pl.multiple_of((side * BLK + column) * TILES, TILES)
            out_ref[z, side * 2 * TILES : (side + 1) * 2 * TILES, :] = rows_ref[pl.ds(first, 2 * TILES), :]


def sums_kernel(weights_ref, counts_ref, wide_ref, column_ref, turned_ref, row_ref, spread_ref):
    def tile_step(tile, carry):
        spread = [jnp.zeros((FOOT, LANES), F32) for _ in range(BAND)]
        rows = []
        for fold in range(FOLDS):
            total = jnp.zeros((FOOT, LANES), F32)
            for lag in range(BAND):
                weights = weights_ref[lag, :, lanes_of(fold, tile)].astype(F32)
                wide_ref[lag, :, lanes_of(fold, tile)] = weights
                spread[lag] = spread[lag] + weights
                total = total + weights
            rows.append(quarter(total))
        row_ref[:, lanes_of(0, tile)] = sum_rows(rows)
        for lag in range(BAND):
            spread_ref[lag, :, lanes_of(0, tile)] = spread[lag]
        return carry

    lax.fori_loop(0, TILES, tile_step, 0)
    for tile, columns in enumerate(fold_lags(spread_ref, counts_ref[...])):
        column_ref[:, tile * LANES : (tile + 1) * LANES] = columns
        turned_ref[:, tile * LANES : (tile + 1) * LANES] = pltpu.roll(columns, SUB, 1)


def rays_kernel(
    place_ref,
    blocks_ref,
    wide_ref,
    counts_ref,
    measured_ref,
    row_ref,
    column_ref,
    turned_ref,
    out_ref,
    window_ref,
    spread_ref,
):
    core, first_block = place_ref[0], place_ref[1]
    first_owner = first_block >> 3
    odd = first_owner & 1
    double = 2 * lax.broadcasted_iota(jnp.int32, (8, LANES), 0)
    covered = [[] for _ in range(TILES)]
    for step in range(2):
        parity = step ^ odd
        side = parity ^ core
        near = double + parity >= first_owner
        turn = (8 - (((first_owner + 1 - parity) >> 1) & 7)) & 7
        for column in range(2):
            for tile in range(TILES):
                rows = blocks_ref[pl.ds((side * 2 + column) * TILES + tile, N_Z, stride=4 * TILES), :]
                covered[tile].append(pltpu.roll(jnp.where(near, rows[0:8], rows[8:16]), turn, 0))
    counts = counts_ref[...]
    window = jnp.concatenate(rotate_each([jnp.concatenate(c, axis=0) for c in covered], counts, True), axis=1)
    window_ref[0] = window
    for lag in range(1, BAND):
        window_ref[lag] = pltpu.roll(window, VOXELS - lag, 1)

    def tile_step(tile, carry):
        lanes = lanes_of(0, tile)
        windows = [window_ref[lag, :, lanes] for lag in range(BAND)]
        rows = []
        for fold in range(FOLDS):
            total = wide_ref[0, :, lanes_of(fold, tile)] * windows[0]
            for lag in range(1, BAND):
                total = total + wide_ref[lag, :, lanes_of(fold, tile)] * windows[lag]
            rows.append(quarter(total))
        residual = (measured_ref[:, lanes] - sum_rows(rows)) / row_ref[:, lanes]
        shares = [residual[fold : fold + 1] for fold in range(FOLDS)]
        for lag in range(BAND):
            spread = wide_ref[lag, :, lanes] * shares[0]
            for fold in range(1, FOLDS):
                spread = spread + wide_ref[lag, :, lanes_of(fold, tile)] * shares[fold]
            spread_ref[lag, :, lanes] = spread
        return carry

    lax.fori_loop(0, TILES, tile_step, 0)
    low = lax.broadcasted_iota(jnp.int32, (HALF, LANES), 1) < SUB
    back = fold_lags(spread_ref, counts)
    for step in range(2):
        parity = step ^ odd
        first = parity * N_VIEW
        base = (((first_owner + 1 - parity) >> 1) << 3) + (first_block & 7)
        base = jnp.full((8, LANES), base, jnp.int32).astype(F32)
        part = slice(step * HALF, (step + 1) * HALF)
        for tile in range(TILES):
            lanes = slice(tile * LANES, (tile + 1) * LANES)
            sums = back[tile][part]
            out_ref[first + 2 * tile, 0:HALF, :] = jnp.where(low, sums, turned_ref[part, lanes])
            out_ref[first + 2 * tile + 1, 0:HALF, :] = jnp.where(low, pltpu.roll(sums, SUB, 1), column_ref[part, lanes])
            out_ref[first + 2 * tile, HALF:MSG, :] = base
            out_ref[first + 2 * tile + 1, HALF:MSG, :] = base


def place_kernel(parts_ref, out_ref):
    lane = lax.broadcasted_iota(jnp.int32, (1, LANES), 1)
    within = ((lane & 7) * BLK + ((lane >> 3) & 1)).astype(F32)
    source = lane >> 4
    targets = []
    for group in range(0, PEERS, 8):
        first = parts_ref[group, HALF : HALF + 1, :]
        for other in range(1, 8):
            first = jnp.where(source == other, parts_ref[group + other, HALF : HALF + 1, :], first)
        targets.append(first + within)
    target = jnp.concatenate(targets, axis=1)
    block = lax.broadcasted_iota(jnp.int32, (N_Z * BLK, PEERS * HALF), 0).astype(F32)
    chosen = jnp.where(block == target, 1.0, 0.0).astype(BF16)
    parts = jnp.concatenate([parts_ref[peer, 0:HALF, :] for peer in range(PEERS)], axis=0)
    high, mid, low = split3(parts)
    both = jnp.dot(chosen, jnp.concatenate([high, mid], axis=1), preferred_element_type=F32)
    total = both[:, :LANES] + (both[:, LANES:] + jnp.dot(chosen, low, preferred_element_type=F32))
    out_ref[...] = total


def finish_kernel(parts_ref, out_ref):
    total = parts_ref[0]
    for z in range(1, N_Z):
        total = total + parts_ref[z]
    columns = pltpu.roll(total, SUB, 1)
    out_ref[...] = (total / jnp.maximum(columns, 1.0))[:, :SUB]


def call(kernel, out_shape, in_specs, scratch=(), cost=None, limit=32):
    return pl.pallas_call(
        kernel,
        out_shape=out_shape,
        in_specs=in_specs,
        out_specs=jax.tree.map(lambda _: VMEM, out_shape),
        scratch_shapes=scratch,
        cost_estimate=cost,
        compiler_params=pltpu.CompilerParams(vmem_limit_bytes=limit * 2**20),
    )


def shards(volume, footprint, offsets, ray_weights, measured):
    member = lax.axis_index("vol")
    core = member & 1
    swap = [(i, i ^ 1) for i in range(2 * N_Z)]
    chips = [[2 * z + c for z in range(N_Z)] for c in range(2)]
    planes = [[z * PEERS + peer for peer in range(PEERS)] for z in range(N_Z)]

    other = lax.ppermute(volume, "vol", swap)
    sent = call(
        pick_kernel,
        jax.ShapeDtypeStruct((N_Z, 4 * TILES, LANES), F32),
        [SMEM, ANY, ANY, VMEM],
        [
            pltpu.VMEM((2 * BLK * TILES, LANES), F32),
            pltpu.VMEM((BLK, VOXELS), F32),
            pltpu.SMEM((2 * N_Z, 1, FOOT), jnp.int32),
            pltpu.SemaphoreType.DMA((2,)),
        ],
    )(core[None], footprint, volume, other)
    blocks = lax.all_to_all(sent, "vol", 0, 0, axis_index_groups=chips)

    weights = ray_weights.reshape(8, 2, 2, BAND, FOLDS * VOXELS)
    weights = jnp.transpose(weights, (3, 1, 2, 0, 4)).reshape(BAND, FOOT, FOLDS * VOXELS)
    counts = jnp.transpose(offsets.reshape(8, 2, 2), (1, 2, 0)).reshape(FOOT, 1)
    counts = jnp.broadcast_to(counts, (FOOT, LANES))
    work = BAND * FOOT * FOLDS * VOXELS
    wide, columns, turned, row_sum = call(
        sums_kernel,
        (
            jax.ShapeDtypeStruct((BAND, FOOT, FOLDS * VOXELS), F32),
            jax.ShapeDtypeStruct((FOOT, VOXELS), F32),
            jax.ShapeDtypeStruct((FOOT, VOXELS), F32),
            jax.ShapeDtypeStruct((FOLDS, VOXELS), F32),
        ),
        [VMEM, VMEM],
        [pltpu.VMEM((BAND, FOOT, VOXELS), F32)],
        pl.CostEstimate(flops=2 * work, bytes_accessed=6 * work, transcendentals=0),
    )(weights, counts)

    first_block = lax.dynamic_index_in_dim(footprint[:, 0, 0], member, 0, keepdims=False)
    parts = call(
        rays_kernel,
        jax.ShapeDtypeStruct((PEERS, MSG, LANES), F32),
        [SMEM] + [VMEM] * 7,
        [pltpu.VMEM((BAND, FOOT, VOXELS), F32), pltpu.VMEM((BAND, FOOT, VOXELS), F32)],
        pl.CostEstimate(flops=4 * work, bytes_accessed=4 * work, transcendentals=0),
    )(
        jnp.stack([core, first_block]),
        blocks.reshape(N_Z * 4 * TILES, LANES),
        wide,
        counts,
        measured.reshape(FOLDS, VOXELS),
        row_sum,
        columns,
        turned,
    )
    parts = lax.all_to_all(parts, ("vol", "view"), 0, 0, axis_index_groups=planes)
    placed = call(place_kernel, jax.ShapeDtypeStruct((N_Z * BLK, LANES), F32), [VMEM])(parts)
    placed = lax.all_to_all(placed.reshape(N_Z, BLK, LANES), "vol", 0, 0, axis_index_groups=chips)
    return call(finish_kernel, jax.ShapeDtypeStruct((BLK, SUB), F32), [VMEM])(placed)


def solution(mesh):
    in_specs = (
        P("vol", None),
        P(None, "view", None),
        P("vol", "view", None),
        P("vol", "view", None, None, None),
        P("vol", "view", None),
    )
    return jax.shard_map(shards, mesh=mesh, in_specs=in_specs, out_specs=P("vol", "view"), check_vma=False)
```

time: 86.6 us -> 81.5 us (0.941)
  blocking collectives: 14.4 us -> 38.7 us
  waiting for transfers between devices: 21.1 us -> 3.47 us
  starting transfers between devices: 35.1 us -> 18.3 us
  local copies, waits for them, and re-layouts: 5.54 us -> 10.9 us
  Pallas kernels: 8.96 us -> 6.54 us
  other arithmetic: 0.83 us -> 2.76 us
    all_to_all x1 -> x2, blocking collectives: 14.4 us -> 38.7 us  [the longest x1 21.6 us: shards(): lax.all_to_all(parts, ('vol', 'view'), 0, 0, axis_index_groups=planes)]
    all_to_all x1 -> x0, waiting for transfers between devices: 12 us -> none  [shards(): lax.all_to_all(placed.reshape(N_Z, 2, BLK, LANES), 'vol', 0, 0, axis_inde...]
    all_to_all x1 -> x0, starting transfers between devices: 10.8 us -> none  [shards(): lax.all_to_all(placed.reshape(N_Z, 2, BLK, LANES), 'vol', 0, 0, axis_inde...]
    ppermute x1 -> x0, starting transfers between devices: 5.92 us -> none  [shards(): lax.ppermute(lax.dynamic_index_in_dim(summed, 1 - core, 0, keepdims=False...]
    all_to_all x1, waiting for transfers between devices: 7.24 us -> 2.43 us  [shards(): blocks = lax.all_to_all(sent, 'vol', 0, 0, axis_index_groups=chips)]
    reshape x0 -> x2, local copies, waits for them, and re-layouts: none -> 2.85 us  [the longest x1 2.76 us: shards(): weights = ray_weights.reshape(8, 2, 2, BAND, FOLDS * VOXELS)]
    pallas_call x4, Pallas kernels: 7.43 us -> 5 us  [the longest x1 2.52 us: shards(): call(rays_kernel, jax.ShapeDtypeStruct((PEERS, MSG, LANES), F32), [SMEM]...]
    unnamed x10 -> x12, local copies, waits for them, and re-layouts: 4.79 us -> 6.63 us
  transfers between devices with their start and end apart: 4 -> 2, of which waited for: 4 -> 2; matrix products, arithmetic and copies ran while one was open for 6% -> 10% of each run, Pallas kernels for 2% -> 2%
where the time goes in v2:
time: 81.5 us; the launch traced here: 80.8 us
  blocking collectives  38.7 us (47%)
  starting transfers between devices  18.3 us (22%)
  local copies, waits for them, and re-layouts  10.9 us (13%)
  Pallas kernels  6.54 us (8%)
  waiting for transfers between devices  3.47 us (4%)
  other arithmetic  2.76 us (3%)
    all_to_all x1, blocking collectives, shards(): lax.all_to_all(parts, ('vol', 'view'), 0, 0, axis_index_groups=planes)  21.6 us
    all_to_all x1, blocking collectives, shards(): lax.all_to_all(placed.reshape(N_Z, BLK, LANES), 'vol', 0, 0, axis_index_g...  17.1 us
    all_to_all x1, starting transfers between devices, shards(): blocks = lax.all_to_all(sent, 'vol', 0, 0, axis_index_groups=chips)  9.55 us
    ppermute x1, starting transfers between devices, shards(): other = lax.ppermute(volume, 'vol', swap)  8.77 us
    unnamed x12, local copies, waits for them, and re-layouts  6.63 us
    reshape x1, local copies, waits for them, and re-layouts, shards(): weights = ray_weights.reshape(8, 2, 2, BAND, FOLDS * VOXELS)  2.76 us
    pallas_call x1, Pallas kernels, shards(): call(rays_kernel, jax.ShapeDtypeStruct((PEERS, MSG, LANES), F32), [SMEM]...  2.52 us
    all_to_all x1, waiting for transfers between devices, shards(): blocks = lax.all_to_all(sent, 'vol', 0, 0, axis_index_groups=chips)  2.43 us
  transfers between devices with their start and end apart: 2, of which 2 were waited for; matrix products, arithmetic and copies ran while one was open for 10% of the time, Pallas kernels for 2%

profile of v2, /device:TPU:1, one launch (start us, length us, event | category | flops | bytes accessed | tf_op | source)
XLA Modules:
  0.0 80.8 jit_solution(12604973599460164009)
XLA Ops:
  0.0 8.8 %collective-permute-start = (f32[8,1024]{1,0:T(8,128)}, f32[8,1024]{1,0:T(8,128)S(1)}, u32[]{:S(2)}, u32[]{:S(2)}) collective-permute-start(f32[8,1024]{1,0:T(8,128)} %own_hbm.1), channel_id=1, source_target_pairs={{0,16},{16,0},{32,48},{48,32},{64,80},{80,64},{96,112},{112,96},{1... | collective-permute-start | bytes 98312 | tf_op jit(solution)/shard_map/ppermute | solution.py:255
  8.8 1.0 %collective-permute-done.other_ref = f32[8,1024]{1,0:T(8,128)S(1)} collective-permute-done((f32[8,1024]{1,0:T(8,128)}, f32[8,1024]{1,0:T(8,128)S(1)}, u32[]{:S(2)}, u32[]{:S(2)}) %collective-permute-start) | collective-permute-done | bytes 32800 | tf_op jit(solution)/shard_map/ppermute | solution.py:255
  9.8 0.0 copy-start.2
  9.8 0.8 copy-done.2
  10.6 0.0 copy-start.3
  10.6 0.7 copy-done.3
  11.3 1.5 %shard_map.55 = f32[16,32,128]{2,1,0:T(8,128)} custom-call(s32[1]{0:T(128)} %bitcast.core_ref, s32[32,1,32]{2,1,0:T(1,128)S(1)} %copy-done.3, f32[8,1024]{1,0:T(8,128)S(1)} %copy-done.2, f32[8,1024]{1,0:T(8,128)S(1)} %collective-permute-done.other_ref), custom_call_target="tpu_custom_call" | custom-call | tf_op jit(solution)/shard_map/pallas_call | solution.py:256
  12.9 9.6 %all-to-all-start = ((f32[16,32,128]{2,1,0:T(8,128)}), f32[16,32,128]{2,1,0:T(8,128)S(1)}, u32[]{:S(2)}, u32[]{:S(2)}) async-start(f32[16,32,128]{2,1,0:T(8,128)} %shard_map.55), calls=%async_computation | async-start | bytes 524288 | tf_op jit(solution)/shard_map/all_to_all | solution.py:267
  22.4 0.5 broadcast.6
  22.9 1.3 %reduce.6 = s32[32]{0:T(128)S(1)} reduce(s32[1,1,32]{2,1,0:T(1,128)} %param.7, s32[]{:T(128)} %broadcast.6), dimensions={0,1}, to_apply=%param.7.reduce_sub_computation.3 | reduce | bytes 260 | tf_op args[2]
  24.2 0.1 reshape.24
  24.3 0.1 copy.9
  24.4 0.1 broadcast_in_dim.8
  24.5 0.0 copy-start.4
  24.5 2.8 %copy.8 = bf16[8,2,2,4,8192]{4,0,2,1,3:T(8,128)(2,1)S(1)} copy(bf16[8,2,2,4,8192]{4,3,2,1,0:T(4,128)(2,1)} %bitcast.14) | data formatting | bytes 4194304 | tf_op jit(solution)/shard_map/reshape | solution.py:269
  27.3 0.5 broadcast.7
  27.8 0.0 copy-done.4
  27.8 0.7 reduce.7
  28.6 1.2 %constant_dynamic-slice_fusion = s32[1,1,1]{2,1,0:T(1,128)} fusion(s32[32,1,1]{2,1,0:T(1,128)} %bitcast.13, s32[]{:T(128)S(6)} %select_n.4), kind=kLoop, calls=%fused_computation.1 | loop fusion | bytes 12 | tf_op jit(solution)/shard_map/jit(dynamic_index_in_dim)/dynamic_slice | solution.py:287
  29.7 0.1 broadcast_in_dim.9.counts_ref
  29.8 1.5 %shard_map.56 = (f32[4,32,8192]{2,1,0:T(8,128)S(1)}, f32[32,1024]{1,0:T(8,128)S(1)}, f32[32,1024]{1,0:T(8,128)S(1)}, f32[8,1024]{1,0:T(8,128)S(1)}) custom-call(bf16[4,32,8192]{2,1,0:T(8,128)(2,1)S(1)} %bitcast.10, s32[32,128]{1,0:T(8,128)S(1)} %broadcast_in_dim.9.counts_ref), custom_call_target="tpu_custom_call" | custom-call | flops 2097152 | bytes 6291456 | tf_op jit(solution)/shard_map/pallas_call | solution.py:274
  31.4 0.0 copy-start
  31.4 1.9 %copy-done = f32[4,32,8192]{2,1,0:T(8,128)} copy-done((f32[4,32,8192]{2,1,0:T(8,128)}, f32[4,32,8192]{2,1,0:T(8,128)S(1)}, u32[]{:S(2)}) %copy-start) | copy-done | bytes 4194328
  33.3 0.7 pad_add_fusion.place_ref
  34.0 2.4 %all-to-all-done = f32[16,32,128]{2,1,0:T(8,128)S(1)} async-done(((f32[16,32,128]{2,1,0:T(8,128)}), f32[16,32,128]{2,1,0:T(8,128)S(1)}, u32[]{:S(2)}, u32[]{:S(2)}) %all-to-all-start) | async-done | bytes 262176 | tf_op jit(solution)/shard_map/all_to_all | solution.py:267
  36.5 0.0 copy-start.1
  36.5 2.2 %copy-done.1 = f32[4,32,8192]{2,1,0:T(8,128)S(1)} copy-done((f32[4,32,8192]{2,1,0:T(8,128)S(1)}, f32[4,32,8192]{2,1,0:T(8,128)}, u32[]{:S(2)}) %copy-start.1) | copy-done | bytes 4194328
  38.6 2.5 %shard_map.57 = f32[32,24,128]{2,1,0:T(8,128)S(1)} custom-call(s32[2]{0:T(128)S(1)} %pad_add_fusion.place_ref, f32[512,128]{1,0:T(8,128)S(1)} %bitcast.11, f32[4,32,8192]{2,1,0:T(8,128)S(1)} %copy-done.1, s32[32,128]{1,0:T(8,128)S(1)} %broadcast_in_dim.9.counts_ref, f32[8,1024]{1,0:T(8,128)S(1)} %reshape.25.measured_ref, ...), custom_call_target="tpu_custom_call" | custom-call | flops 4194304 | bytes 4194304 | tf_op jit(solution)/shard_map/pallas_call | solution.py:288
  41.2 21.6 %all_to_all.15.parts_ref = f32[32,24,128]{2,1,0:T(8,128)S(1)} all-to-all(f32[32,24,128]{2,1,0:T(8,128)S(1)} %shard_map.57), channel_id=1, replica_groups={{0,1,2,3,4,5,6,7,8,9,10,11,12,13,14,15,16,17,18,19,20,21,22,23,24,25,26..., dimensions={0} | all-to-all | bytes 786432 | tf_op jit(solution)/shard_map/all_to_all | solution.py:304
  62.7 0.2 shard_map.58
  63.0 17.1 %all_to_all.16.parts_ref = f32[16,8,128]{2,1,0:T(8,128)S(1)} all-to-all(f32[16,8,128]{2,1,0:T(8,128)S(1)} %bitcast.12), channel_id=1, replica_groups={{0,32,64,96,128,160,192,224,256,288,320,352,384,416,448,480},{16,48,80,..., dimensions={0} | all-to-all | bytes 131072 | tf_op jit(solution)/shard_map/all_to_all | solution.py:306
  80.1 0.7 shard_map.59
  (1 shorter events, 0.0 us)
Async XLA Ops:
  0.0 9.8 %collective-permute-start = (f32[8,1024]{1,0:T(8,128)}, f32[8,1024]{1,0:T(8,128)S(1)}, u32[]{:S(2)}, u32[]{:S(2)}) collective-permute-start(f32[8,1024]{1,0:T(8,128)} %own_hbm.1), channel_id=1, source_target_pairs={{0,16},{16,0},{32,48},{48,32},{64,80},{80,64},{96,112},{112,96},{1... | collective-permute-start | bytes 98312 | tf_op jit(solution)/shard_map/ppermute | solution.py:255
  9.8 0.8 copy-start.2
  10.6 0.7 copy-start.3
  12.9 23.6 %all-to-all-start = ((f32[16,32,128]{2,1,0:T(8,128)}), f32[16,32,128]{2,1,0:T(8,128)S(1)}, u32[]{:S(2)}, u32[]{:S(2)}) async-start(f32[16,32,128]{2,1,0:T(8,128)} %shard_map.55), calls=%async_computation | async-start | bytes 524288 | tf_op jit(solution)/shard_map/all_to_all | solution.py:267
  24.5 3.3 %copy-start.4 = (f32[1,1,8192]{2,1,0:T(1,128)S(1)}, f32[1,1,8192]{2,1,0:T(1,128)}, u32[]{:S(2)}) copy-start(f32[1,1,8192]{2,1,0:T(1,128)} %param.9) | copy-start | bytes 98308
  31.4 1.9 %copy-start = (f32[4,32,8192]{2,1,0:T(8,128)}, f32[4,32,8192]{2,1,0:T(8,128)S(1)}, u32[]{:S(2)}) copy-start(f32[4,32,8192]{2,1,0:T(8,128)S(1)} %get-tuple-element.9.wide_ref) | copy-start | bytes 12582916
  36.5 2.2 %copy-start.1 = (f32[4,32,8192]{2,1,0:T(8,128)S(1)}, f32[4,32,8192]{2,1,0:T(8,128)}, u32[]{:S(2)}) copy-start(f32[4,32,8192]{2,1,0:T(8,128)} %copy-done) | copy-start | bytes 12582916

commit v3 on v2

--- a/solution.py
+++ b/solution.py
@@ -18,10 +18,12 @@
 PEERS = 2 * N_VIEW
 MSG = HALF + 8
 SUB = VOXELS // N_VIEW
+FIRST_Z = 8
+FIRST_VIEW = 10
 
 VMEM = pl.BlockSpec(memory_space=pltpu.VMEM)
 SMEM = pl.BlockSpec(memory_space=pltpu.SMEM)
-ANY = pl.BlockSpec(memory_space=pl.ANY)
+HBM = pl.BlockSpec(memory_space=pltpu.HBM)
 F32 = jnp.float32
 BF16 = jnp.bfloat16
 
@@ -88,6 +90,8 @@
 
 
 def lanes_of(fold, tile):
+    if isinstance(tile, int):
+        return slice(fold * VOXELS + tile * LANES, fold * VOXELS + (tile + 1) * LANES)
     return pl.ds(pl.multiple_of(fold * VOXELS + tile * LANES, LANES), LANES)
 
 
@@ -110,10 +114,10 @@
         column = foot_ref[2 * z + core, 0, 0] & (BLK - 1)
         for side in range(2):
             first = pl.multiple_of((side * BLK + column) * TILES, TILES)
-            out_ref[z, side * 2 * TILES : (side + 1) * 2 * TILES, :] = rows_ref[pl.ds(first, 2 * TILES), :]
-
-
-def sums_kernel(weights_ref, counts_ref, wide_ref, column_ref, turned_ref, row_ref, spread_ref):
+            out_ref[z ^ FIRST_Z, side * 2 * TILES : (side + 1) * 2 * TILES, :] = rows_ref[pl.ds(first, 2 * TILES), :]
+
+
+def sums_kernel(weights_ref, counts_ref, column_ref, turned_ref, row_ref, spread_ref):
     def tile_step(tile, carry):
         spread = [jnp.zeros((FOOT, LANES), F32) for _ in range(BAND)]
         rows = []
@@ -121,7 +125,6 @@
             total = jnp.zeros((FOOT, LANES), F32)
             for lag in range(BAND):
                 weights = weights_ref[lag, :, lanes_of(fold, tile)].astype(F32)
-                wide_ref[lag, :, lanes_of(fold, tile)] = weights
                 spread[lag] = spread[lag] + weights
                 total = total + weights
             rows.append(quarter(total))
@@ -139,7 +142,7 @@
 def rays_kernel(
     place_ref,
     blocks_ref,
-    wide_ref,
+    weights_ref,
     counts_ref,
     measured_ref,
     row_ref,
@@ -148,6 +151,7 @@
     out_ref,
     window_ref,
     spread_ref,
+    share_ref,
 ):
     core, first_block = place_ref[0], place_ref[1]
     first_owner = first_block >> 3
@@ -162,47 +166,47 @@
         for column in range(2):
             for tile in range(TILES):
                 rows = blocks_ref[pl.ds((side * 2 + column) * TILES + tile, N_Z, stride=4 * TILES), :]
-                covered[tile].append(pltpu.roll(jnp.where(near, rows[0:8], rows[8:16]), turn, 0))
+                covered[tile].append(pltpu.roll(jnp.where(near, rows[8:16], rows[0:8]), turn, 0))
     counts = counts_ref[...]
     window = jnp.concatenate(rotate_each([jnp.concatenate(c, axis=0) for c in covered], counts, True), axis=1)
     window_ref[0] = window
     for lag in range(1, BAND):
         window_ref[lag] = pltpu.roll(window, VOXELS - lag, 1)
 
-    def tile_step(tile, carry):
+    for tile in range(TILES):
         lanes = lanes_of(0, tile)
         windows = [window_ref[lag, :, lanes] for lag in range(BAND)]
         rows = []
         for fold in range(FOLDS):
-            total = wide_ref[0, :, lanes_of(fold, tile)] * windows[0]
+            total = weights_ref[0, :, lanes_of(fold, tile)].astype(F32) * windows[0]
             for lag in range(1, BAND):
-                total = total + wide_ref[lag, :, lanes_of(fold, tile)] * windows[lag]
+                total = total + weights_ref[lag, :, lanes_of(fold, tile)].astype(F32) * windows[lag]
             rows.append(quarter(total))
-        residual = (measured_ref[:, lanes] - sum_rows(rows)) / row_ref[:, lanes]
-        shares = [residual[fold : fold + 1] for fold in range(FOLDS)]
+        share_ref[:, lanes] = (measured_ref[:, lanes] - sum_rows(rows)) / row_ref[:, lanes]
+    for tile in range(TILES):
+        lanes = lanes_of(0, tile)
         for lag in range(BAND):
-            spread = wide_ref[lag, :, lanes] * shares[0]
+            spread = weights_ref[lag, :, lanes].astype(F32) * share_ref[0:1, lanes]
             for fold in range(1, FOLDS):
-                spread = spread + wide_ref[lag, :, lanes_of(fold, tile)] * shares[fold]
+                spread = spread + weights_ref[lag, :, lanes_of(fold, tile)].astype(F32) * share_ref[fold : fold + 1, lanes]
             spread_ref[lag, :, lanes] = spread
-        return carry
-
-    lax.fori_loop(0, TILES, tile_step, 0)
     low = lax.broadcasted_iota(jnp.int32, (HALF, LANES), 1) < SUB
     back = fold_lags(spread_ref, counts)
     for step in range(2):
         parity = step ^ odd
         first = parity * N_VIEW
+        even = [first + (2 * tile ^ FIRST_VIEW) for tile in range(TILES)]
+        other = [first + (2 * tile + 1 ^ FIRST_VIEW) for tile in range(TILES)]
         base = (((first_owner + 1 - parity) >> 1) << 3) + (first_block & 7)
         base = jnp.full((8, LANES), base, jnp.int32).astype(F32)
         part = slice(step * HALF, (step + 1) * HALF)
         for tile in range(TILES):
             lanes = slice(tile * LANES, (tile + 1) * LANES)
             sums = back[tile][part]
-            out_ref[first + 2 * tile, 0:HALF, :] = jnp.where(low, sums, turned_ref[part, lanes])
-            out_ref[first + 2 * tile + 1, 0:HALF, :] = jnp.where(low, pltpu.roll(sums, SUB, 1), column_ref[part, lanes])
-            out_ref[first + 2 * tile, HALF:MSG, :] = base
-            out_ref[first + 2 * tile + 1, HALF:MSG, :] = base
+            out_ref[even[tile], 0:HALF, :] = jnp.where(low, sums, turned_ref[part, lanes])
+            out_ref[other[tile], 0:HALF, :] = jnp.where(low, pltpu.roll(sums, SUB, 1), column_ref[part, lanes])
+            out_ref[even[tile], HALF:MSG, :] = base
+            out_ref[other[tile], HALF:MSG, :] = base
 
 
 def place_kernel(parts_ref, out_ref):
@@ -216,7 +220,8 @@
             first = jnp.where(source == other, parts_ref[group + other, HALF : HALF + 1, :], first)
         targets.append(first + within)
     target = jnp.concatenate(targets, axis=1)
-    block = lax.broadcasted_iota(jnp.int32, (N_Z * BLK, PEERS * HALF), 0).astype(F32)
+    block = lax.broadcasted_iota(jnp.int32, (N_Z * BLK, PEERS * HALF), 0)
+    block = (block ^ (FIRST_Z * BLK)).astype(F32)
     chosen = jnp.where(block == target, 1.0, 0.0).astype(BF16)
     parts = jnp.concatenate([parts_ref[peer, 0:HALF, :] for peer in range(PEERS)], axis=0)
     high, mid, low = split3(parts)
@@ -233,7 +238,7 @@
     out_ref[...] = (total / jnp.maximum(columns, 1.0))[:, :SUB]
 
 
-def call(kernel, out_shape, in_specs, scratch=(), cost=None, limit=32):
+def call(kernel, out_shape, in_specs, scratch=(), cost=None, limit=16):
     return pl.pallas_call(
         kernel,
         out_shape=out_shape,
@@ -249,14 +254,14 @@
     member = lax.axis_index("vol")
     core = member & 1
     swap = [(i, i ^ 1) for i in range(2 * N_Z)]
-    chips = [[2 * z + c for z in range(N_Z)] for c in range(2)]
-    planes = [[z * PEERS + peer for peer in range(PEERS)] for z in range(N_Z)]
+    chips = [[2 * (z ^ FIRST_Z) + c for z in range(N_Z)] for c in range(2)]
+    planes = [[z * PEERS + (peer ^ FIRST_VIEW) for peer in range(PEERS)] for z in range(N_Z)]
 
     other = lax.ppermute(volume, "vol", swap)
     sent = call(
         pick_kernel,
         jax.ShapeDtypeStruct((N_Z, 4 * TILES, LANES), F32),
-        [SMEM, ANY, ANY, VMEM],
+        [SMEM, HBM, HBM, VMEM],
         [
             pltpu.VMEM((2 * BLK * TILES, LANES), F32),
             pltpu.VMEM((BLK, VOXELS), F32),
@@ -271,17 +276,16 @@
     counts = jnp.transpose(offsets.reshape(8, 2, 2), (1, 2, 0)).reshape(FOOT, 1)
     counts = jnp.broadcast_to(counts, (FOOT, LANES))
     work = BAND * FOOT * FOLDS * VOXELS
-    wide, columns, turned, row_sum = call(
+    columns, turned, row_sum = call(
         sums_kernel,
         (
-            jax.ShapeDtypeStruct((BAND, FOOT, FOLDS * VOXELS), F32),
             jax.ShapeDtypeStruct((FOOT, VOXELS), F32),
             jax.ShapeDtypeStruct((FOOT, VOXELS), F32),
             jax.ShapeDtypeStruct((FOLDS, VOXELS), F32),
         ),
         [VMEM, VMEM],
         [pltpu.VMEM((BAND, FOOT, VOXELS), F32)],
-        pl.CostEstimate(flops=2 * work, bytes_accessed=6 * work, transcendentals=0),
+        pl.CostEstimate(flops=2 * work, bytes_accessed=2 * work, transcendentals=0),
     )(weights, counts)
 
     first_block = lax.dynamic_index_in_dim(footprint[:, 0, 0], member, 0, keepdims=False)
@@ -289,12 +293,16 @@
         rays_kernel,
         jax.ShapeDtypeStruct((PEERS, MSG, LANES), F32),
         [SMEM] + [VMEM] * 7,
-        [pltpu.VMEM((BAND, FOOT, VOXELS), F32), pltpu.VMEM((BAND, FOOT, VOXELS), F32)],
-        pl.CostEstimate(flops=4 * work, bytes_accessed=4 * work, transcendentals=0),
+        [
+            pltpu.VMEM((BAND, FOOT, VOXELS), F32),
+            pltpu.VMEM((BAND, FOOT, VOXELS), F32),
+            pltpu.VMEM((FOLDS, VOXELS), F32),
+        ],
+        pl.CostEstimate(flops=4 * work, bytes_accessed=2 * work, transcendentals=0),
     )(
         jnp.stack([core, first_block]),
         blocks.reshape(N_Z * 4 * TILES, LANES),
-        wide,
+        weights,
         counts,
         measured.reshape(FOLDS, VOXELS),
         row_sum,

time: 81.5 us -> 71.9 us (0.88)
  blocking collectives: 38.7 us -> 30 us
  local copies, waits for them, and re-layouts: 10.9 us -> 6.78 us
  starting transfers between devices: 18.3 us -> 21.7 us
    all_to_all x1, blocking collectives: 21.6 us -> 14.6 us  [shards(): lax.all_to_all(parts, ('vol', 'view'), 0, 0, axis_index_groups=planes)]
    unnamed x12 -> x6, local copies, waits for them, and re-layouts: 6.63 us -> 2.51 us
    all_to_all x1, starting transfers between devices: 9.55 us -> 12.9 us  [shards(): blocks = lax.all_to_all(sent, 'vol', 0, 0, axis_index_groups=chips)]
    all_to_all x1, blocking collectives: 17.1 us -> 15.3 us  [shards(): lax.all_to_all(placed.reshape(N_Z, BLK, LANES), 'vol', 0, 0, axis_index_g...]
  transfers between devices with their start and end apart: 2 -> 2, of which waited for: 2 -> 2; matrix products, arithmetic and copies ran while one was open for 10% -> 12% of each run, Pallas kernels for 2% -> 2%
where the time goes in v3:
time: 71.9 us; the launch traced here: 71.3 us
  blocking collectives  30 us (42%)
  starting transfers between devices  21.7 us (30%)
  local copies, waits for them, and re-layouts  6.78 us (9%)
  Pallas kernels  5.81 us (8%)
  other arithmetic  3.52 us (5%)
  waiting for transfers between devices  3.47 us (5%)
    all_to_all x1, blocking collectives, shards(): lax.all_to_all(placed.reshape(N_Z, BLK, LANES), 'vol', 0, 0, axis_index_g...  15.3 us
    all_to_all x1, blocking collectives, shards(): lax.all_to_all(parts, ('vol', 'view'), 0, 0, axis_index_groups=planes)  14.6 us
    all_to_all x1, starting transfers between devices, shards(): blocks = lax.all_to_all(sent, 'vol', 0, 0, axis_index_groups=chips)  12.9 us
    ppermute x1, starting transfers between devices, shards(): other = lax.ppermute(volume, 'vol', swap)  8.77 us
    unnamed x2, other arithmetic  2.8 us
    reshape x1, local copies, waits for them, and re-layouts, shards(): weights = ray_weights.reshape(8, 2, 2, BAND, FOLDS * VOXELS)  2.74 us
    unnamed x6, local copies, waits for them, and re-layouts  2.51 us
    all_to_all x1, waiting for transfers between devices, shards(): blocks = lax.all_to_all(sent, 'vol', 0, 0, axis_index_groups=chips)  2.43 us
  transfers between devices with their start and end apart: 2, of which 2 were waited for; matrix products, arithmetic and copies ran while one was open for 12% of the time, Pallas kernels for 2%

profile of v3, /device:TPU:1, one launch (start us, length us, event | category | flops | bytes accessed | tf_op | source)
XLA Modules:
  0.0 71.3 jit_solution(12673848062732337757)
XLA Ops:
  0.0 8.8 %collective-permute-start = (f32[8,1024]{1,0:T(8,128)}, f32[8,1024]{1,0:T(8,128)S(1)}, u32[]{:S(2)}, u32[]{:S(2)}) collective-permute-start(f32[8,1024]{1,0:T(8,128)} %own_hbm.1), channel_id=1, source_target_pairs={{0,16},{16,0},{32,48},{48,32},{64,80},{80,64},{96,112},{112,96},{1... | collective-permute-start | bytes 98312 | tf_op jit(solution)/shard_map/ppermute | solution.py:260
  8.8 1.0 %collective-permute-done.other_ref = f32[8,1024]{1,0:T(8,128)S(1)} collective-permute-done((f32[8,1024]{1,0:T(8,128)}, f32[8,1024]{1,0:T(8,128)S(1)}, u32[]{:S(2)}, u32[]{:S(2)}) %collective-permute-start) | collective-permute-done | bytes 32800 | tf_op jit(solution)/shard_map/ppermute | solution.py:260
  9.8 0.0 copy-start
  9.8 0.8 %copy-done = f32[8,1024]{1,0:T(8,128)S(1)} copy-done((f32[8,1024]{1,0:T(8,128)S(1)}, f32[8,1024]{1,0:T(8,128)}, u32[]{:S(2)}) %copy-start) | copy-done | bytes 32792
  10.6 0.0 copy-start.1
  10.6 0.7 %copy-done.1 = s32[32,1,32]{2,1,0:T(1,128)S(1)} copy-done((s32[32,1,32]{2,1,0:T(1,128)S(1)}, s32[32,1,32]{2,1,0:T(1,128)}, u32[]{:S(2)}) %copy-start.1) | copy-done | bytes 4120
  11.3 1.5 %shard_map.55 = f32[16,32,128]{2,1,0:T(8,128)} custom-call(s32[1]{0:T(128)} %bitcast.core_ref, s32[32,1,32]{2,1,0:T(1,128)S(1)} %copy-done.1, f32[8,1024]{1,0:T(8,128)S(1)} %copy-done, f32[8,1024]{1,0:T(8,128)S(1)} %collective-permute-done.other_ref), custom_call_target="tpu_custom_call" | custom-call | tf_op jit(solution)/shard_map/pallas_call | solution.py:261
  12.9 12.9 %all-to-all-start = ((f32[16,32,128]{2,1,0:T(8,128)}), f32[16,32,128]{2,1,0:T(8,128)S(1)}, u32[]{:S(2)}, u32[]{:S(2)}) async-start(f32[16,32,128]{2,1,0:T(8,128)} %shard_map.55), calls=%async_computation | async-start | bytes 524288 | tf_op jit(solution)/shard_map/all_to_all | solution.py:272
  25.8 0.5 broadcast.6
  26.3 1.3 %reduce.6 = s32[32]{0:T(128)S(1)} reduce(s32[1,1,32]{2,1,0:T(1,128)} %param.7, s32[]{:T(128)} %broadcast.6), dimensions={0,1}, to_apply=%param.7.reduce_sub_computation.3 | reduce | bytes 260 | tf_op args[2]
  27.6 0.1 reshape.24
  27.7 0.1 copy.9
  27.8 0.1 broadcast_in_dim.8
  27.9 0.5 broadcast.7
  28.4 1.5 %reduce.7 = f32[8192]{0:T(1024)S(1)} reduce(f32[1,1,8192]{2,1,0:T(1,128)} %param.9, f32[]{:T(128)} %broadcast.7), dimensions={0,1}, to_apply=%param.9.reduce_sub_computation.3 | reduce | bytes 65540 | tf_op args[4]
  29.9 2.7 %copy.8 = bf16[8,2,2,4,8192]{4,0,2,1,3:T(8,128)(2,1)S(1)} copy(bf16[8,2,2,4,8192]{4,3,2,1,0:T(4,128)(2,1)} %bitcast.15) | data formatting | bytes 4194304 | tf_op jit(solution)/shard_map/reshape | solution.py:274
  32.7 1.2 %constant_dynamic-slice_fusion = s32[1,1,1]{2,1,0:T(1,128)} fusion(s32[32,1,1]{2,1,0:T(1,128)} %bitcast.14, s32[]{:T(128)S(6)} %select_n.4), kind=kLoop, calls=%fused_computation.1 | loop fusion | bytes 12 | tf_op jit(solution)/shard_map/jit(dynamic_index_in_dim)/dynamic_slice | solution.py:291
  33.8 0.1 broadcast_in_dim.9.counts_ref
  33.9 1.4 %shard_map.56 = (f32[32,1024]{1,0:T(8,128)S(1)}, f32[32,1024]{1,0:T(8,128)S(1)}, f32[8,1024]{1,0:T(8,128)S(1)}) custom-call(bf16[4,32,8192]{2,1,0:T(8,128)(2,1)S(1)} %bitcast.10, s32[32,128]{1,0:T(8,128)S(1)} %broadcast_in_dim.9.counts_ref), custom_call_target="tpu_custom_call" | custom-call | flops 2097152 | bytes 2097152 | tf_op jit(solution)/shard_map/pallas_call | solution.py:279
  35.4 0.7 %pad_add_fusion.place_ref = s32[2]{0:T(128)S(1)} fusion(s32[1]{0:T(128)} %bitcast.1, s32[1]{0:T(128)} %bitcast.core_ref), kind=kLoop, calls=%fused_computation | loop fusion | flops 2 | bytes 16 | tf_op jit(solution)/shard_map/stack | solution.py:303
  36.1 2.4 %all-to-all-done = f32[16,32,128]{2,1,0:T(8,128)S(1)} async-done(((f32[16,32,128]{2,1,0:T(8,128)}), f32[16,32,128]{2,1,0:T(8,128)S(1)}, u32[]{:S(2)}, u32[]{:S(2)}) %all-to-all-start) | async-done | bytes 262176 | tf_op jit(solution)/shard_map/all_to_all | solution.py:272
  38.5 1.9 %shard_map.57 = f32[32,24,128]{2,1,0:T(8,128)S(1)} custom-call(s32[2]{0:T(128)S(1)} %pad_add_fusion.place_ref, f32[512,128]{1,0:T(8,128)S(1)} %bitcast.12, bf16[4,32,8192]{2,1,0:T(8,128)(2,1)S(1)} %bitcast.11, s32[32,128]{1,0:T(8,128)S(1)} %broadcast_in_dim.9.counts_ref, f32[8,1024]{1,0:T(8,128)S(1)} %reshape.25.measured_ref, ...), custom_call_target="tpu_custom_call" | custom-call | flops 4194304 | bytes 2097152 | tf_op jit(solution)/shard_map/pallas_call | solution.py:292
  40.4 14.6 %all_to_all.15.parts_ref = f32[32,24,128]{2,1,0:T(8,128)S(1)} all-to-all(f32[32,24,128]{2,1,0:T(8,128)S(1)} %shard_map.57), channel_id=1, replica_groups={{10,11,8,9,14,15,12,13,2,3,0,1,6,7,4,5,26,27,24,25,30,31,28,29,18,19,16..., dimensions={0} | all-to-all | bytes 786432 | tf_op jit(solution)/shard_map/all_to_all | solution.py:312
  55.0 0.2 shard_map.58
  55.3 15.3 %all_to_all.16.parts_ref = f32[16,8,128]{2,1,0:T(8,128)S(1)} all-to-all(f32[16,8,128]{2,1,0:T(8,128)S(1)} %bitcast.13), channel_id=1, replica_groups={{256,288,320,352,384,416,448,480,0,32,64,96,128,160,192,224},{272,304,3..., dimensions={0} | all-to-all | bytes 131072 | tf_op jit(solution)/shard_map/all_to_all | solution.py:314
  70.6 0.7 shard_map.59
  (1 shorter events, 0.0 us)
Async XLA Ops:
  0.0 9.8 %collective-permute-start = (f32[8,1024]{1,0:T(8,128)}, f32[8,1024]{1,0:T(8,128)S(1)}, u32[]{:S(2)}, u32[]{:S(2)}) collective-permute-start(f32[8,1024]{1,0:T(8,128)} %own_hbm.1), channel_id=1, source_target_pairs={{0,16},{16,0},{32,48},{48,32},{64,80},{80,64},{96,112},{112,96},{1... | collective-permute-start | bytes 98312 | tf_op jit(solution)/shard_map/ppermute | solution.py:260
  9.8 0.8 %copy-start = (f32[8,1024]{1,0:T(8,128)S(1)}, f32[8,1024]{1,0:T(8,128)}, u32[]{:S(2)}) copy-start(f32[8,1024]{1,0:T(8,128)} %own_hbm.1) | copy-start | bytes 98308
  10.6 0.7 %copy-start.1 = (s32[32,1,32]{2,1,0:T(1,128)S(1)}, s32[32,1,32]{2,1,0:T(1,128)}, u32[]{:S(2)}) copy-start(s32[32,1,32]{2,1,0:T(1,128)} %foot_hbm.1) | copy-start | bytes 12292
  12.9 25.7 %all-to-all-start = ((f32[16,32,128]{2,1,0:T(8,128)}), f32[16,32,128]{2,1,0:T(8,128)S(1)}, u32[]{:S(2)}, u32[]{:S(2)}) async-start(f32[16,32,128]{2,1,0:T(8,128)} %shard_map.55), calls=%async_computation | async-start | bytes 524288 | tf_op jit(solution)/shard_map/all_to_all | solution.py:272

commit v4 on v3

--- a/solution.py
+++ b/solution.py
@@ -18,12 +18,12 @@
 PEERS = 2 * N_VIEW
 MSG = HALF + 8
 SUB = VOXELS // N_VIEW
-FIRST_Z = 8
+FIRST_OUT = 11
+FIRST_BACK = 8
 FIRST_VIEW = 10
 
 VMEM = pl.BlockSpec(memory_space=pltpu.VMEM)
 SMEM = pl.BlockSpec(memory_space=pltpu.SMEM)
-HBM = pl.BlockSpec(memory_space=pltpu.HBM)
 F32 = jnp.float32
 BF16 = jnp.bfloat16
 
@@ -95,26 +95,35 @@
     return pl.ds(pl.multiple_of(fold * VOXELS + tile * LANES, LANES), LANES)
 
 
-def pick_kernel(core_ref, foot_hbm, own_hbm, other_ref, out_ref, rows_ref, own_ref, foot_ref, sems):
-    foot_copy = pltpu.make_async_copy(foot_hbm, foot_ref, sems.at[0])
-    own_copy = pltpu.make_async_copy(own_hbm, own_ref, sems.at[1])
-    foot_copy.start()
-    own_copy.start()
+def spread_rows(rows_ref, ref):
+    for tile in range(TILES):
+        rows_ref[pl.ds(tile, BLK, stride=TILES), :] = ref[:, tile * LANES : (tile + 1) * LANES]
+
+
+def own_kernel(core_ref, foot_ref, own_ref, half_ref, column_ref, rows_ref):
     core = core_ref[0]
-
-    def spread_rows(side, ref):
-        for tile in range(TILES):
-            rows_ref[pl.ds(side * BLK * TILES + tile, BLK, stride=TILES), :] = ref[:, tile * LANES : (tile + 1) * LANES]
-
-    spread_rows(1, other_ref)
-    own_copy.wait()
-    spread_rows(0, own_ref)
-    foot_copy.wait()
+    spread_rows(rows_ref, own_ref)
     for z in range(N_Z):
         column = foot_ref[2 * z + core, 0, 0] & (BLK - 1)
-        for side in range(2):
-            first = pl.multiple_of((side * BLK + column) * TILES, TILES)
-            out_ref[z ^ FIRST_Z, side * 2 * TILES : (side + 1) * 2 * TILES, :] = rows_ref[pl.ds(first, 2 * TILES), :]
+        place = (z - FIRST_OUT) % N_Z
+        first = pl.multiple_of(column * TILES, TILES)
+        half_ref[place] = rows_ref[pl.ds(first, 2 * TILES), :]
+        column_ref[place] = jnp.full((TILES, LANES), column, jnp.int32)
+
+
+def other_kernel(half_ref, column_ref, other_ref, sent_ref, rows_ref):
+    spread_rows(rows_ref, other_ref)
+    rows = [rows_ref[block * TILES : (block + 1) * TILES, :] for block in range(BLK)]
+    for place in range(N_Z):
+        column = column_ref[place]
+        one, two = rows[0], rows[1]
+        for block in range(1, BLK - 1):
+            chosen = column == block
+            one = jnp.where(chosen, rows[block], one)
+            two = jnp.where(chosen, rows[block + 1], two)
+        sent_ref[place, 0 : 2 * TILES, :] = half_ref[place]
+        sent_ref[place, 2 * TILES : 3 * TILES, :] = one
+        sent_ref[place, 3 * TILES : 4 * TILES, :] = two
 
 
 def sums_kernel(weights_ref, counts_ref, column_ref, turned_ref, row_ref, spread_ref):
@@ -156,17 +165,18 @@
     core, first_block = place_ref[0], place_ref[1]
     first_owner = first_block >> 3
     odd = first_owner & 1
-    double = 2 * lax.broadcasted_iota(jnp.int32, (8, LANES), 0)
+    double = 2 * ((lax.broadcasted_iota(jnp.int32, (8, LANES), 0) + FIRST_OUT) & (N_Z - 1))
     covered = [[] for _ in range(TILES)]
     for step in range(2):
         parity = step ^ odd
         side = parity ^ core
-        near = double + parity >= first_owner
-        turn = (8 - (((first_owner + 1 - parity) >> 1) & 7)) & 7
+        owner = double + parity - first_owner
+        near = (owner >= 0) & (owner < N_Z)
+        turn = (FIRST_OUT - ((first_owner + 1 - parity) >> 1)) & 7
         for column in range(2):
             for tile in range(TILES):
                 rows = blocks_ref[pl.ds((side * 2 + column) * TILES + tile, N_Z, stride=4 * TILES), :]
-                covered[tile].append(pltpu.roll(jnp.where(near, rows[8:16], rows[0:8]), turn, 0))
+                covered[tile].append(pltpu.roll(jnp.where(near, rows[0:8], rows[8:16]), turn, 0))
     counts = counts_ref[...]
     window = jnp.concatenate(rotate_each([jnp.concatenate(c, axis=0) for c in covered], counts, True), axis=1)
     window_ref[0] = window
@@ -221,7 +231,7 @@
         targets.append(first + within)
     target = jnp.concatenate(targets, axis=1)
     block = lax.broadcasted_iota(jnp.int32, (N_Z * BLK, PEERS * HALF), 0)
-    block = (block ^ (FIRST_Z * BLK)).astype(F32)
+    block = ((block + FIRST_BACK * BLK) & (N_Z * BLK - 1)).astype(F32)
     chosen = jnp.where(block == target, 1.0, 0.0).astype(BF16)
     parts = jnp.concatenate([parts_ref[peer, 0:HALF, :] for peer in range(PEERS)], axis=0)
     high, mid, low = split3(parts)
@@ -238,7 +248,7 @@
     out_ref[...] = (total / jnp.maximum(columns, 1.0))[:, :SUB]
 
 
-def call(kernel, out_shape, in_specs, scratch=(), cost=None, limit=16):
+def call(kernel, out_shape, in_specs, scratch=(), cost=None):
     return pl.pallas_call(
         kernel,
         out_shape=out_shape,
@@ -246,7 +256,7 @@
         out_specs=jax.tree.map(lambda _: VMEM, out_shape),
         scratch_shapes=scratch,
         cost_estimate=cost,
-        compiler_params=pltpu.CompilerParams(vmem_limit_bytes=limit * 2**20),
+        compiler_params=pltpu.CompilerParams(vmem_limit_bytes=16 * 2**20),
     )
 
 
@@ -254,22 +264,29 @@
     member = lax.axis_index("vol")
     core = member & 1
     swap = [(i, i ^ 1) for i in range(2 * N_Z)]
-    chips = [[2 * (z ^ FIRST_Z) + c for z in range(N_Z)] for c in range(2)]
+    out_chips, back_chips = (
+        [[2 * ((z + first) % N_Z) + c for z in range(N_Z)] for c in range(2)] for first in (FIRST_OUT, FIRST_BACK)
+    )
     planes = [[z * PEERS + (peer ^ FIRST_VIEW) for peer in range(PEERS)] for z in range(N_Z)]
 
     other = lax.ppermute(volume, "vol", swap)
+    rows_scratch = pltpu.VMEM((BLK * TILES, LANES), F32)
+    half, chosen = call(
+        own_kernel,
+        (
+            jax.ShapeDtypeStruct((N_Z, 2 * TILES, LANES), F32),
+            jax.ShapeDtypeStruct((N_Z, TILES, LANES), jnp.int32),
+        ),
+        [SMEM, SMEM, VMEM],
+        [rows_scratch],
+    )(core[None], footprint, volume)
     sent = call(
-        pick_kernel,
+        other_kernel,
         jax.ShapeDtypeStruct((N_Z, 4 * TILES, LANES), F32),
-        [SMEM, HBM, HBM, VMEM],
-        [
-            pltpu.VMEM((2 * BLK * TILES, LANES), F32),
-            pltpu.VMEM((BLK, VOXELS), F32),
-            pltpu.SMEM((2 * N_Z, 1, FOOT), jnp.int32),
-            pltpu.SemaphoreType.DMA((2,)),
-        ],
-    )(core[None], footprint, volume, other)
-    blocks = lax.all_to_all(sent, "vol", 0, 0, axis_index_groups=chips)
+        [VMEM] * 3,
+        [rows_scratch],
+    )(half, chosen, other)
+    blocks = lax.all_to_all(sent, "vol", 0, 0, axis_index_groups=out_chips)
 
     weights = ray_weights.reshape(8, 2, 2, BAND, FOLDS * VOXELS)
     weights = jnp.transpose(weights, (3, 1, 2, 0, 4)).reshape(BAND, FOOT, FOLDS * VOXELS)
@@ -311,7 +328,7 @@
     )
     parts = lax.all_to_all(parts, ("vol", "view"), 0, 0, axis_index_groups=planes)
     placed = call(place_kernel, jax.ShapeDtypeStruct((N_Z * BLK, LANES), F32), [VMEM])(parts)
-    placed = lax.all_to_all(placed.reshape(N_Z, BLK, LANES), "vol", 0, 0, axis_index_groups=chips)
+    placed = lax.all_to_all(placed.reshape(N_Z, BLK, LANES), "vol", 0, 0, axis_index_groups=back_chips)
     return call(finish_kernel, jax.ShapeDtypeStruct((BLK, SUB), F32), [VMEM])(placed)
 
 

time: 71.9 us -> 70.7 us (0.983)
  starting transfers between devices: 21.7 us -> 19 us
  waiting for transfers between devices: 3.47 us -> 4.41 us
    all_to_all x1, starting transfers between devices: 12.9 us -> 10.2 us  [shards(): blocks = lax.all_to_all(sent, 'vol', 0, 0, axis_index_groups=out_chips)]
    all_to_all x1, waiting for transfers between devices: 2.43 us -> 4.41 us  [shards(): blocks = lax.all_to_all(sent, 'vol', 0, 0, axis_index_groups=out_chips)]
    ppermute x1, waiting for transfers between devices: 1.04 us -> 0.01 us  [shards(): other = lax.ppermute(volume, 'vol', swap)]
    pallas_call x1 -> x2, Pallas kernels: 1.54 us -> 1.57 us  [the longest x1 0.83 us: shards(): call(own_kernel, (jax.ShapeDtypeStruct((N_Z, 2 * TILES, LANES), F32), jax...]
  transfers between devices with their start and end apart: 2 -> 2, of which waited for: 2 -> 1; matrix products, arithmetic and copies ran while one was open for 12% -> 13% of each run, Pallas kernels for 2% -> 3%
where the time goes in v4:
time: 70.7 us; the launch traced here: 70.1 us
  blocking collectives  30.5 us (43%)
  starting transfers between devices  19 us (27%)
  local copies, waits for them, and re-layouts  6.77 us (10%)
  Pallas kernels  5.85 us (8%)
  waiting for transfers between devices  4.41 us (6%)
  other arithmetic  3.52 us (5%)
    all_to_all x1, blocking collectives, shards(): lax.all_to_all(placed.reshape(N_Z, BLK, LANES), 'vol', 0, 0, axis_index_g...  15.3 us
    all_to_all x1, blocking collectives, shards(): lax.all_to_all(parts, ('vol', 'view'), 0, 0, axis_index_groups=planes)  15.2 us
    all_to_all x1, starting transfers between devices, shards(): blocks = lax.all_to_all(sent, 'vol', 0, 0, axis_index_groups=out_chips)  10.2 us
    ppermute x1, starting transfers between devices, shards(): other = lax.ppermute(volume, 'vol', swap)  8.77 us
    all_to_all x1, waiting for transfers between devices, shards(): blocks = lax.all_to_all(sent, 'vol', 0, 0, axis_index_groups=out_chips)  4.41 us
    unnamed x2, other arithmetic  2.8 us
    reshape x1, local copies, waits for them, and re-layouts, shards(): weights = ray_weights.reshape(8, 2, 2, BAND, FOLDS * VOXELS)  2.74 us
    unnamed x6, local copies, waits for them, and re-layouts  2.5 us
  transfers between devices with their start and end apart: 2, of which 1 were waited for; matrix products, arithmetic and copies ran while one was open for 13% of the time, Pallas kernels for 3%

profile of v4, /device:TPU:1, one launch (start us, length us, event | category | flops | bytes accessed | tf_op | source)
XLA Modules:
  0.0 70.1 jit_solution(8842110765708652994)
XLA Ops:
  0.0 8.8 %collective-permute-start = (f32[8,1024]{1,0:T(8,128)}, f32[8,1024]{1,0:T(8,128)S(1)}, u32[]{:S(2)}, u32[]{:S(2)}) collective-permute-start(f32[8,1024]{1,0:T(8,128)} %own_ref.1), channel_id=1, source_target_pairs={{0,16},{16,0},{32,48},{48,32},{64,80},{80,64},{96,112},{112,96},{1... | collective-permute-start | bytes 98312 | tf_op jit(solution)/shard_map/ppermute | solution.py:272
  8.8 0.0 copy-start
  8.8 0.7 %copy-done = f32[8,1024]{1,0:T(8,128)S(1)} copy-done((f32[8,1024]{1,0:T(8,128)S(1)}, f32[8,1024]{1,0:T(8,128)}, u32[]{:S(2)}) %copy-start) | copy-done | bytes 32792
  9.5 0.0 copy-start.1
  9.6 0.7 %copy-done.1 = s32[32,1,32]{2,1,0:T(1,128)S(1)} copy-done((s32[32,1,32]{2,1,0:T(1,128)S(1)}, s32[32,1,32]{2,1,0:T(1,128)}, u32[]{:S(2)}) %copy-start.1) | copy-done | bytes 4120
  10.3 0.8 %shard_map.55 = (f32[16,16,128]{2,1,0:T(8,128)S(1)}, s32[16,8,128]{2,1,0:T(8,128)S(1)}) custom-call(s32[1]{0:T(128)} %bitcast.core_ref, s32[32,1,32]{2,1,0:T(1,128)S(1)} %copy-done.1, f32[8,1024]{1,0:T(8,128)S(1)} %copy-done), custom_call_target="tpu_custom_call" | custom-call | tf_op jit(solution)/shard_map/pallas_call | solution.py:274
  11.1 0.0 collective-permute-done.other_ref
  11.1 0.7 %shard_map.56 = f32[16,32,128]{2,1,0:T(8,128)} custom-call(f32[16,16,128]{2,1,0:T(8,128)S(1)} %get-tuple-element.10.half_ref, s32[16,8,128]{2,1,0:T(8,128)S(1)} %get-tuple-element.11.column_ref, f32[8,1024]{1,0:T(8,128)S(1)} %collective-permute-done.other_ref), custom_call_target="tpu_custom_call" | custom-call | tf_op jit(solution)/shard_map/pallas_call | solution.py:283
  11.9 10.2 %all-to-all-start = ((f32[16,32,128]{2,1,0:T(8,128)}), f32[16,32,128]{2,1,0:T(8,128)S(1)}, u32[]{:S(2)}, u32[]{:S(2)}) async-start(f32[16,32,128]{2,1,0:T(8,128)} %shard_map.56), calls=%async_computation | async-start | bytes 524288 | tf_op jit(solution)/shard_map/all_to_all | solution.py:289
  22.1 0.5 broadcast.6
  22.6 1.3 %reduce.6 = s32[32]{0:T(128)S(1)} reduce(s32[1,1,32]{2,1,0:T(1,128)} %param.7, s32[]{:T(128)} %broadcast.6), dimensions={0,1}, to_apply=%param.7.reduce_sub_computation.3 | reduce | bytes 260 | tf_op args[2]
  23.9 0.1 reshape.24
  24.0 0.1 copy.9
  24.1 0.1 broadcast_in_dim.8
  24.2 0.5 broadcast.7
  24.7 1.5 %reduce.7 = f32[8192]{0:T(1024)S(1)} reduce(f32[1,1,8192]{2,1,0:T(1,128)} %param.9, f32[]{:T(128)} %broadcast.7), dimensions={0,1}, to_apply=%param.9.reduce_sub_computation.3 | reduce | bytes 65540 | tf_op args[4]
  26.2 2.7 %copy.8 = bf16[8,2,2,4,8192]{4,0,2,1,3:T(8,128)(2,1)S(1)} copy(bf16[8,2,2,4,8192]{4,3,2,1,0:T(4,128)(2,1)} %bitcast.15) | data formatting | bytes 4194304 | tf_op jit(solution)/shard_map/reshape | solution.py:291
  29.0 1.2 %constant_dynamic-slice_fusion = s32[1,1,1]{2,1,0:T(1,128)} fusion(s32[32,1,1]{2,1,0:T(1,128)} %bitcast.14, s32[]{:T(128)S(6)} %select_n.4), kind=kLoop, calls=%fused_computation.1 | loop fusion | bytes 12 | tf_op jit(solution)/shard_map/jit(dynamic_index_in_dim)/dynamic_slice | solution.py:308
  30.1 0.1 broadcast_in_dim.9.counts_ref
  30.2 1.4 %shard_map.57 = (f32[32,1024]{1,0:T(8,128)S(1)}, f32[32,1024]{1,0:T(8,128)S(1)}, f32[8,1024]{1,0:T(8,128)S(1)}) custom-call(bf16[4,32,8192]{2,1,0:T(8,128)(2,1)S(1)} %bitcast.10, s32[32,128]{1,0:T(8,128)S(1)} %broadcast_in_dim.9.counts_ref), custom_call_target="tpu_custom_call" | custom-call | flops 2097152 | bytes 2097152 | tf_op jit(solution)/shard_map/pallas_call | solution.py:296
  31.6 0.7 %pad_add_fusion.place_ref = s32[2]{0:T(128)S(1)} fusion(s32[1]{0:T(128)} %bitcast.1, s32[1]{0:T(128)} %bitcast.core_ref), kind=kLoop, calls=%fused_computation | loop fusion | flops 2 | bytes 16 | tf_op jit(solution)/shard_map/stack | solution.py:320
  32.4 4.4 %all-to-all-done = f32[16,32,128]{2,1,0:T(8,128)S(1)} async-done(((f32[16,32,128]{2,1,0:T(8,128)}), f32[16,32,128]{2,1,0:T(8,128)S(1)}, u32[]{:S(2)}, u32[]{:S(2)}) %all-to-all-start) | async-done | bytes 262176 | tf_op jit(solution)/shard_map/all_to_all | solution.py:289
  36.8 1.9 %shard_map.58 = f32[32,24,128]{2,1,0:T(8,128)S(1)} custom-call(s32[2]{0:T(128)S(1)} %pad_add_fusion.place_ref, f32[512,128]{1,0:T(8,128)S(1)} %bitcast.12, bf16[4,32,8192]{2,1,0:T(8,128)(2,1)S(1)} %bitcast.11, s32[32,128]{1,0:T(8,128)S(1)} %broadcast_in_dim.9.counts_ref, f32[8,1024]{1,0:T(8,128)S(1)} %reshape.25.measured_ref, ...), custom_call_target="tpu_custom_call" | custom-call | flops 4194304 | bytes 2097152 | tf_op jit(solution)/shard_map/pallas_call | solution.py:309
  38.7 15.2 %all_to_all.15.parts_ref = f32[32,24,128]{2,1,0:T(8,128)S(1)} all-to-all(f32[32,24,128]{2,1,0:T(8,128)S(1)} %shard_map.58), channel_id=1, replica_groups={{10,11,8,9,14,15,12,13,2,3,0,1,6,7,4,5,26,27,24,25,30,31,28,29,18,19,16..., dimensions={0} | all-to-all | bytes 786432 | tf_op jit(solution)/shard_map/all_to_all | solution.py:329
  53.9 0.2 shard_map.59
  54.1 15.3 %all_to_all.16.parts_ref = f32[16,8,128]{2,1,0:T(8,128)S(1)} all-to-all(f32[16,8,128]{2,1,0:T(8,128)S(1)} %bitcast.13), channel_id=1, replica_groups={{256,288,320,352,384,416,448,480,0,32,64,96,128,160,192,224},{272,304,3..., dimensions={0} | all-to-all | bytes 131072 | tf_op jit(solution)/shard_map/all_to_all | solution.py:331
  69.5 0.7 shard_map.60
  (1 shorter events, 0.0 us)
Async XLA Ops:
  0.0 11.1 %collective-permute-start = (f32[8,1024]{1,0:T(8,128)}, f32[8,1024]{1,0:T(8,128)S(1)}, u32[]{:S(2)}, u32[]{:S(2)}) collective-permute-start(f32[8,1024]{1,0:T(8,128)} %own_ref.1), channel_id=1, source_target_pairs={{0,16},{16,0},{32,48},{48,32},{64,80},{80,64},{96,112},{112,96},{1... | collective-permute-start | bytes 98312 | tf_op jit(solution)/shard_map/ppermute | solution.py:272
  8.8 0.8 %copy-start = (f32[8,1024]{1,0:T(8,128)S(1)}, f32[8,1024]{1,0:T(8,128)}, u32[]{:S(2)}) copy-start(f32[8,1024]{1,0:T(8,128)} %own_ref.1) | copy-start | bytes 98308
  9.5 0.7 %copy-start.1 = (s32[32,1,32]{2,1,0:T(1,128)S(1)}, s32[32,1,32]{2,1,0:T(1,128)}, u32[]{:S(2)}) copy-start(s32[32,1,32]{2,1,0:T(1,128)} %foot_ref.1) | copy-start | bytes 12292
  11.9 24.9 %all-to-all-start = ((f32[16,32,128]{2,1,0:T(8,128)}), f32[16,32,128]{2,1,0:T(8,128)S(1)}, u32[]{:S(2)}, u32[]{:S(2)}) async-start(f32[16,32,128]{2,1,0:T(8,128)} %shard_map.56), calls=%async_computation | async-start | bytes 524288 | tf_op jit(solution)/shard_map/all_to_all | solution.py:289

commit v5 on v4

--- a/solution.py
+++ b/solution.py
@@ -19,7 +19,7 @@
 MSG = HALF + 8
 SUB = VOXELS // N_VIEW
 FIRST_OUT = 11
-FIRST_BACK = 8
+FIRST_BACK = 9
 FIRST_VIEW = 10
 
 VMEM = pl.BlockSpec(memory_space=pltpu.VMEM)
@@ -95,24 +95,7 @@
     return pl.ds(pl.multiple_of(fold * VOXELS + tile * LANES, LANES), LANES)
 
 
-def spread_rows(rows_ref, ref):
-    for tile in range(TILES):
-        rows_ref[pl.ds(tile, BLK, stride=TILES), :] = ref[:, tile * LANES : (tile + 1) * LANES]
-
-
-def own_kernel(core_ref, foot_ref, own_ref, half_ref, column_ref, rows_ref):
-    core = core_ref[0]
-    spread_rows(rows_ref, own_ref)
-    for z in range(N_Z):
-        column = foot_ref[2 * z + core, 0, 0] & (BLK - 1)
-        place = (z - FIRST_OUT) % N_Z
-        first = pl.multiple_of(column * TILES, TILES)
-        half_ref[place] = rows_ref[pl.ds(first, 2 * TILES), :]
-        column_ref[place] = jnp.full((TILES, LANES), column, jnp.int32)
-
-
-def other_kernel(half_ref, column_ref, other_ref, sent_ref, rows_ref):
-    spread_rows(rows_ref, other_ref)
+def pick_pairs(rows_ref, column_ref, out_ref, first):
     rows = [rows_ref[block * TILES : (block + 1) * TILES, :] for block in range(BLK)]
     for place in range(N_Z):
         column = column_ref[place]
@@ -121,9 +104,27 @@
             chosen = column == block
             one = jnp.where(chosen, rows[block], one)
             two = jnp.where(chosen, rows[block + 1], two)
+        out_ref[place, first : first + TILES, :] = one
+        out_ref[place, first + TILES : first + 2 * TILES, :] = two
+
+
+def own_kernel(core_ref, foot_ref, own_ref, half_ref, column_ref, rows_ref):
+    core = core_ref[0]
+    for z in range(N_Z):
+        place = (z - FIRST_OUT) % N_Z
+        first = foot_ref[2 * z + core] & (BLK - 1)
+        column_ref[place] = jnp.broadcast_to(first[:, 0:1], (TILES, LANES))
+    for tile in range(TILES):
+        rows_ref[pl.ds(tile, BLK, stride=TILES), :] = own_ref[:, tile * LANES : (tile + 1) * LANES]
+    pick_pairs(rows_ref, column_ref, half_ref, 0)
+
+
+def other_kernel(half_ref, column_ref, other_ref, sent_ref, rows_ref):
+    for tile in range(TILES):
+        rows_ref[pl.ds(tile, BLK, stride=TILES), :] = other_ref[:, tile * LANES : (tile + 1) * LANES]
+    for place in range(N_Z):
         sent_ref[place, 0 : 2 * TILES, :] = half_ref[place]
-        sent_ref[place, 2 * TILES : 3 * TILES, :] = one
-        sent_ref[place, 3 * TILES : 4 * TILES, :] = two
+    pick_pairs(rows_ref, column_ref, sent_ref, 2 * TILES)
 
 
 def sums_kernel(weights_ref, counts_ref, column_ref, turned_ref, row_ref, spread_ref):
@@ -277,7 +278,7 @@
             jax.ShapeDtypeStruct((N_Z, 2 * TILES, LANES), F32),
             jax.ShapeDtypeStruct((N_Z, TILES, LANES), jnp.int32),
         ),
-        [SMEM, SMEM, VMEM],
+        [SMEM, VMEM, VMEM],
         [rows_scratch],
     )(core[None], footprint, volume)
     sent = call(

time: 70.7 us -> 69.7 us (0.986)
  Pallas kernels: 5.85 us -> 5.13 us
    pallas_call x1, Pallas kernels: 0.83 us -> 0.11 us  [shards(): call(own_kernel, (jax.ShapeDtypeStruct((N_Z, 2 * TILES, LANES), F32), jax...]
  transfers between devices with their start and end apart: 2 -> 2, of which waited for: 1 -> 1; matrix products, arithmetic and copies ran while one was open for 13% -> 13% of each run, Pallas kernels for 3% -> 2%
where the time goes in v5:
time: 69.7 us; the launch traced here: 69.2 us
  blocking collectives  30.2 us (43%)
  starting transfers between devices  19 us (27%)
  local copies, waits for them, and re-layouts  6.77 us (10%)
  Pallas kernels  5.13 us (7%)
  waiting for transfers between devices  4.41 us (6%)
  other arithmetic  3.52 us (5%)
    all_to_all x1, blocking collectives, shards(): lax.all_to_all(parts, ('vol', 'view'), 0, 0, axis_index_groups=planes)  15.2 us
    all_to_all x1, blocking collectives, shards(): lax.all_to_all(placed.reshape(N_Z, BLK, LANES), 'vol', 0, 0, axis_index_g...  15.1 us
    all_to_all x1, starting transfers between devices, shards(): blocks = lax.all_to_all(sent, 'vol', 0, 0, axis_index_groups=out_chips)  10.2 us
    ppermute x1, starting transfers between devices, shards(): other = lax.ppermute(volume, 'vol', swap)  8.77 us
    all_to_all x1, waiting for transfers between devices, shards(): blocks = lax.all_to_all(sent, 'vol', 0, 0, axis_index_groups=out_chips)  4.41 us
    unnamed x2, other arithmetic  2.8 us
    reshape x1, local copies, waits for them, and re-layouts, shards(): weights = ray_weights.reshape(8, 2, 2, BAND, FOLDS * VOXELS)  2.74 us
    unnamed x6, local copies, waits for them, and re-layouts  2.5 us
  transfers between devices with their start and end apart: 2, of which 1 were waited for; matrix products, arithmetic and copies ran while one was open for 13% of the time, Pallas kernels for 2%

profile of v5, /device:TPU:1, one launch (start us, length us, event | category | flops | bytes accessed | tf_op | source)
XLA Modules:
  0.0 69.2 jit_solution(16545623965730656140)
XLA Ops:
  0.0 8.8 %collective-permute-start = (f32[8,1024]{1,0:T(8,128)}, f32[8,1024]{1,0:T(8,128)S(1)}, u32[]{:S(2)}, u32[]{:S(2)}) collective-permute-start(f32[8,1024]{1,0:T(8,128)} %own_ref.1), channel_id=1, source_target_pairs={{0,16},{16,0},{32,48},{48,32},{64,80},{80,64},{96,112},{112,96},{1... | collective-permute-start | bytes 98312 | tf_op jit(solution)/shard_map/ppermute | solution.py:273
  8.8 0.0 copy-start
  8.8 0.7 %copy-done = f32[8,1024]{1,0:T(8,128)S(1)} copy-done((f32[8,1024]{1,0:T(8,128)S(1)}, f32[8,1024]{1,0:T(8,128)}, u32[]{:S(2)}) %copy-start) | copy-done | bytes 32792
  9.5 0.0 copy-start.1
  9.6 0.7 %copy-done.1 = s32[32,1,32]{2,1,0:T(1,128)S(1)} copy-done((s32[32,1,32]{2,1,0:T(1,128)S(1)}, s32[32,1,32]{2,1,0:T(1,128)}, u32[]{:S(2)}) %copy-start.1) | copy-done | bytes 4120
  10.3 0.1 shard_map.55
  10.4 0.0 collective-permute-done.other_ref
  10.4 0.7 %shard_map.56 = f32[16,32,128]{2,1,0:T(8,128)} custom-call(f32[16,16,128]{2,1,0:T(8,128)S(1)} %get-tuple-element.10.half_ref, s32[16,8,128]{2,1,0:T(8,128)S(1)} %get-tuple-element.11.column_ref, f32[8,1024]{1,0:T(8,128)S(1)} %collective-permute-done.other_ref), custom_call_target="tpu_custom_call" | custom-call | tf_op jit(solution)/shard_map/pallas_call | solution.py:284
  11.1 10.2 %all-to-all-start = ((f32[16,32,128]{2,1,0:T(8,128)}), f32[16,32,128]{2,1,0:T(8,128)S(1)}, u32[]{:S(2)}, u32[]{:S(2)}) async-start(f32[16,32,128]{2,1,0:T(8,128)} %shard_map.56), calls=%async_computation | async-start | bytes 524288 | tf_op jit(solution)/shard_map/all_to_all | solution.py:290
  21.4 0.5 broadcast.6
  21.9 1.3 %reduce.6 = s32[32]{0:T(128)S(1)} reduce(s32[1,1,32]{2,1,0:T(1,128)} %param.7, s32[]{:T(128)} %broadcast.6), dimensions={0,1}, to_apply=%param.7.reduce_sub_computation.3 | reduce | bytes 260 | tf_op args[2]
  23.2 0.1 reshape.24
  23.3 0.1 copy.9
  23.4 0.1 broadcast_in_dim.8
  23.5 0.5 broadcast.7
  24.0 1.5 %reduce.7 = f32[8192]{0:T(1024)S(1)} reduce(f32[1,1,8192]{2,1,0:T(1,128)} %param.9, f32[]{:T(128)} %broadcast.7), dimensions={0,1}, to_apply=%param.9.reduce_sub_computation.3 | reduce | bytes 65540 | tf_op args[4]
  25.5 2.7 %copy.8 = bf16[8,2,2,4,8192]{4,0,2,1,3:T(8,128)(2,1)S(1)} copy(bf16[8,2,2,4,8192]{4,3,2,1,0:T(4,128)(2,1)} %bitcast.15) | data formatting | bytes 4194304 | tf_op jit(solution)/shard_map/reshape | solution.py:292
  28.2 1.2 %constant_dynamic-slice_fusion = s32[1,1,1]{2,1,0:T(1,128)} fusion(s32[32,1,1]{2,1,0:T(1,128)} %bitcast.14, s32[]{:T(128)S(6)} %select_n.4), kind=kLoop, calls=%fused_computation.1 | loop fusion | bytes 12 | tf_op jit(solution)/shard_map/jit(dynamic_index_in_dim)/dynamic_slice | solution.py:309
  29.4 0.1 broadcast_in_dim.9.counts_ref
  29.5 1.4 %shard_map.57 = (f32[32,1024]{1,0:T(8,128)S(1)}, f32[32,1024]{1,0:T(8,128)S(1)}, f32[8,1024]{1,0:T(8,128)S(1)}) custom-call(bf16[4,32,8192]{2,1,0:T(8,128)(2,1)S(1)} %bitcast.10, s32[32,128]{1,0:T(8,128)S(1)} %broadcast_in_dim.9.counts_ref), custom_call_target="tpu_custom_call" | custom-call | flops 2097152 | bytes 2097152 | tf_op jit(solution)/shard_map/pallas_call | solution.py:297
  30.9 0.7 %pad_add_fusion.place_ref = s32[2]{0:T(128)S(1)} fusion(s32[1]{0:T(128)} %bitcast.1, s32[1]{0:T(128)} %bitcast.core_ref), kind=kLoop, calls=%fused_computation | loop fusion | flops 2 | bytes 16 | tf_op jit(solution)/shard_map/stack | solution.py:321
  31.7 4.4 %all-to-all-done = f32[16,32,128]{2,1,0:T(8,128)S(1)} async-done(((f32[16,32,128]{2,1,0:T(8,128)}), f32[16,32,128]{2,1,0:T(8,128)S(1)}, u32[]{:S(2)}, u32[]{:S(2)}) %all-to-all-start) | async-done | bytes 262176 | tf_op jit(solution)/shard_map/all_to_all | solution.py:290
  36.1 1.9 %shard_map.58 = f32[32,24,128]{2,1,0:T(8,128)S(1)} custom-call(s32[2]{0:T(128)S(1)} %pad_add_fusion.place_ref, f32[512,128]{1,0:T(8,128)S(1)} %bitcast.12, bf16[4,32,8192]{2,1,0:T(8,128)(2,1)S(1)} %bitcast.11, s32[32,128]{1,0:T(8,128)S(1)} %broadcast_in_dim.9.counts_ref, f32[8,1024]{1,0:T(8,128)S(1)} %reshape.25.measured_ref, ...), custom_call_target="tpu_custom_call" | custom-call | flops 4194304 | bytes 2097152 | tf_op jit(solution)/shard_map/pallas_call | solution.py:310
  38.0 15.2 %all_to_all.15.parts_ref = f32[32,24,128]{2,1,0:T(8,128)S(1)} all-to-all(f32[32,24,128]{2,1,0:T(8,128)S(1)} %shard_map.58), channel_id=1, replica_groups={{10,11,8,9,14,15,12,13,2,3,0,1,6,7,4,5,26,27,24,25,30,31,28,29,18,19,16..., dimensions={0} | all-to-all | bytes 786432 | tf_op jit(solution)/shard_map/all_to_all | solution.py:330
  53.1 0.2 shard_map.59
  53.4 15.1 %all_to_all.16.parts_ref = f32[16,8,128]{2,1,0:T(8,128)S(1)} all-to-all(f32[16,8,128]{2,1,0:T(8,128)S(1)} %bitcast.13), channel_id=1, replica_groups={{288,320,352,384,416,448,480,0,32,64,96,128,160,192,224,256},{304,336,3..., dimensions={0} | all-to-all | bytes 131072 | tf_op jit(solution)/shard_map/all_to_all | solution.py:332
  68.5 0.7 shard_map.60
  (1 shorter events, 0.0 us)
Async XLA Ops:
  0.0 10.4 %collective-permute-start = (f32[8,1024]{1,0:T(8,128)}, f32[8,1024]{1,0:T(8,128)S(1)}, u32[]{:S(2)}, u32[]{:S(2)}) collective-permute-start(f32[8,1024]{1,0:T(8,128)} %own_ref.1), channel_id=1, source_target_pairs={{0,16},{16,0},{32,48},{48,32},{64,80},{80,64},{96,112},{112,96},{1... | collective-permute-start | bytes 98312 | tf_op jit(solution)/shard_map/ppermute | solution.py:273
  8.8 0.8 %copy-start = (f32[8,1024]{1,0:T(8,128)S(1)}, f32[8,1024]{1,0:T(8,128)}, u32[]{:S(2)}) copy-start(f32[8,1024]{1,0:T(8,128)} %own_ref.1) | copy-start | bytes 98308
  9.5 0.7 %copy-start.1 = (s32[32,1,32]{2,1,0:T(1,128)S(1)}, s32[32,1,32]{2,1,0:T(1,128)}, u32[]{:S(2)}) copy-start(s32[32,1,32]{2,1,0:T(1,128)} %foot_ref.1) | copy-start | bytes 12292
  11.1 24.9 %all-to-all-start = ((f32[16,32,128]{2,1,0:T(8,128)}), f32[16,32,128]{2,1,0:T(8,128)S(1)}, u32[]{:S(2)}, u32[]{:S(2)}) async-start(f32[16,32,128]{2,1,0:T(8,128)} %shard_map.56), calls=%async_computation | async-start | bytes 524288 | tf_op jit(solution)/shard_map/all_to_all | solution.py:290

commit v6 on v5

--- a/solution.py
+++ b/solution.py
@@ -16,11 +16,14 @@
 N_Z = 16
 N_VIEW = 16
 PEERS = 2 * N_VIEW
-MSG = HALF + 8
+PIECE = 2
+PIECES = HALF // PIECE
 SUB = VOXELS // N_VIEW
 FIRST_OUT = 11
 FIRST_BACK = 9
 FIRST_VIEW = 10
+STEP_OUT = 9
+STEP_BACK = 1
 
 VMEM = pl.BlockSpec(memory_space=pltpu.VMEM)
 SMEM = pl.BlockSpec(memory_space=pltpu.SMEM)
@@ -111,7 +114,7 @@
 def own_kernel(core_ref, foot_ref, own_ref, half_ref, column_ref, rows_ref):
     core = core_ref[0]
     for z in range(N_Z):
-        place = (z - FIRST_OUT) % N_Z
+        place = STEP_OUT * (z - FIRST_OUT) % N_Z
         first = foot_ref[2 * z + core] & (BLK - 1)
         column_ref[place] = jnp.broadcast_to(first[:, 0:1], (TILES, LANES))
     for tile in range(TILES):
@@ -147,6 +150,12 @@
     for tile, columns in enumerate(fold_lags(spread_ref, counts_ref[...])):
         column_ref[:, tile * LANES : (tile + 1) * LANES] = columns
         turned_ref[:, tile * LANES : (tile + 1) * LANES] = pltpu.roll(columns, SUB, 1)
+
+
+def message(out_ref, peer, rows, base):
+    for piece in range(PIECES):
+        out_ref[peer, piece] = rows[piece * PIECE : (piece + 1) * PIECE]
+    out_ref[peer, PIECES] = base
 
 
 def rays_kernel(
@@ -166,7 +175,7 @@
     core, first_block = place_ref[0], place_ref[1]
     first_owner = first_block >> 3
     odd = first_owner & 1
-    double = 2 * ((lax.broadcasted_iota(jnp.int32, (8, LANES), 0) + FIRST_OUT) & (N_Z - 1))
+    double = 2 * ((lax.broadcasted_iota(jnp.int32, (8, LANES), 0) * STEP_OUT + FIRST_OUT) & (N_Z - 1))
     covered = [[] for _ in range(TILES)]
     for step in range(2):
         parity = step ^ odd
@@ -209,15 +218,13 @@
         even = [first + (2 * tile ^ FIRST_VIEW) for tile in range(TILES)]
         other = [first + (2 * tile + 1 ^ FIRST_VIEW) for tile in range(TILES)]
         base = (((first_owner + 1 - parity) >> 1) << 3) + (first_block & 7)
-        base = jnp.full((8, LANES), base, jnp.int32).astype(F32)
+        base = jnp.full((PIECE, LANES), base, jnp.int32).astype(F32)
         part = slice(step * HALF, (step + 1) * HALF)
         for tile in range(TILES):
             lanes = slice(tile * LANES, (tile + 1) * LANES)
             sums = back[tile][part]
-            out_ref[even[tile], 0:HALF, :] = jnp.where(low, sums, turned_ref[part, lanes])
-            out_ref[other[tile], 0:HALF, :] = jnp.where(low, pltpu.roll(sums, SUB, 1), column_ref[part, lanes])
-            out_ref[even[tile], HALF:MSG, :] = base
-            out_ref[other[tile], HALF:MSG, :] = base
+            message(out_ref, even[tile], jnp.where(low, sums, turned_ref[part, lanes]), base)
+            message(out_ref, other[tile], jnp.where(low, pltpu.roll(sums, SUB, 1), column_ref[part, lanes]), base)
 
 
 def place_kernel(parts_ref, out_ref):
@@ -226,15 +233,16 @@
     source = lane >> 4
     targets = []
     for group in range(0, PEERS, 8):
-        first = parts_ref[group, HALF : HALF + 1, :]
+        first = parts_ref[group, PIECES, 0:1, :]
         for other in range(1, 8):
-            first = jnp.where(source == other, parts_ref[group + other, HALF : HALF + 1, :], first)
+            first = jnp.where(source == other, parts_ref[group + other, PIECES, 0:1, :], first)
         targets.append(first + within)
     target = jnp.concatenate(targets, axis=1)
     block = lax.broadcasted_iota(jnp.int32, (N_Z * BLK, PEERS * HALF), 0)
-    block = ((block + FIRST_BACK * BLK) & (N_Z * BLK - 1)).astype(F32)
+    chip = ((block >> 3) * STEP_BACK + FIRST_BACK) & (N_Z - 1)
+    block = (chip * BLK + (block & (BLK - 1))).astype(F32)
     chosen = jnp.where(block == target, 1.0, 0.0).astype(BF16)
-    parts = jnp.concatenate([parts_ref[peer, 0:HALF, :] for peer in range(PEERS)], axis=0)
+    parts = jnp.concatenate([parts_ref[peer, piece] for peer in range(PEERS) for piece in range(PIECES)], axis=0)
     high, mid, low = split3(parts)
     both = jnp.dot(chosen, jnp.concatenate([high, mid], axis=1), preferred_element_type=F32)
     total = both[:, :LANES] + (both[:, LANES:] + jnp.dot(chosen, low, preferred_element_type=F32))
@@ -266,7 +274,8 @@
     core = member & 1
     swap = [(i, i ^ 1) for i in range(2 * N_Z)]
     out_chips, back_chips = (
-        [[2 * ((z + first) % N_Z) + c for z in range(N_Z)] for c in range(2)] for first in (FIRST_OUT, FIRST_BACK)
+        [[2 * ((step * place + first) % N_Z) + c for place in range(N_Z)] for c in range(2)]
+        for first, step in ((FIRST_OUT, STEP_OUT), (FIRST_BACK, STEP_BACK))
     )
     planes = [[z * PEERS + (peer ^ FIRST_VIEW) for peer in range(PEERS)] for z in range(N_Z)]
 
@@ -309,7 +318,7 @@
     first_block = lax.dynamic_index_in_dim(footprint[:, 0, 0], member, 0, keepdims=False)
     parts = call(
         rays_kernel,
-        jax.ShapeDtypeStruct((PEERS, MSG, LANES), F32),
+        jax.ShapeDtypeStruct((PEERS, PIECES + 1, PIECE, LANES), F32),
         [SMEM] + [VMEM] * 7,
         [
             pltpu.VMEM((BAND, FOOT, VOXELS), F32),

time: 69.7 us -> 68.5 us (0.983)
  blocking collectives: 30.2 us -> 29 us
    all_to_all x1, blocking collectives: 15.2 us -> 14.1 us  [shards(): lax.all_to_all(parts, ('vol', 'view'), 0, 0, axis_index_groups=planes)]
where the time goes in v6:
time: 68.5 us; the launch traced here: 68 us
  blocking collectives  29 us (42%)
  starting transfers between devices  19 us (28%)
  local copies, waits for them, and re-layouts  6.77 us (10%)
  Pallas kernels  5.19 us (8%)
  waiting for transfers between devices  4.39 us (6%)
  other arithmetic  3.52 us (5%)
    all_to_all x1, blocking collectives, shards(): lax.all_to_all(placed.reshape(N_Z, BLK, LANES), 'vol', 0, 0, axis_index_g...  14.9 us
    all_to_all x1, blocking collectives, shards(): lax.all_to_all(parts, ('vol', 'view'), 0, 0, axis_index_groups=planes)  14.1 us
    all_to_all x1, starting transfers between devices, shards(): blocks = lax.all_to_all(sent, 'vol', 0, 0, axis_index_groups=out_chips)  10.2 us
    ppermute x1, starting transfers between devices, shards(): other = lax.ppermute(volume, 'vol', swap)  8.77 us
    all_to_all x1, waiting for transfers between devices, shards(): blocks = lax.all_to_all(sent, 'vol', 0, 0, axis_index_groups=out_chips)  4.38 us
    unnamed x2, other arithmetic  2.8 us
    reshape x1, local copies, waits for them, and re-layouts, shards(): weights = ray_weights.reshape(8, 2, 2, BAND, FOLDS * VOXELS)  2.74 us
    unnamed x6, local copies, waits for them, and re-layouts  2.5 us
  transfers between devices with their start and end apart: 2, of which 1 were waited for; matrix products, arithmetic and copies ran while one was open for 13% of the time, Pallas kernels for 2%

profile of v6, /device:TPU:1, one launch (start us, length us, event | category | flops | bytes accessed | tf_op | source)
XLA Modules:
  0.0 68.0 jit_solution(17061340167629249223)
XLA Ops:
  0.0 8.8 %collective-permute-start = (f32[8,1024]{1,0:T(8,128)}, f32[8,1024]{1,0:T(8,128)S(1)}, u32[]{:S(2)}, u32[]{:S(2)}) collective-permute-start(f32[8,1024]{1,0:T(8,128)} %own_ref.1), channel_id=1, source_target_pairs={{0,16},{16,0},{32,48},{48,32},{64,80},{80,64},{96,112},{112,96},{1... | collective-permute-start | bytes 98312 | tf_op jit(solution)/shard_map/ppermute | solution.py:282
  8.8 0.0 copy-start
  8.8 0.7 %copy-done = f32[8,1024]{1,0:T(8,128)S(1)} copy-done((f32[8,1024]{1,0:T(8,128)S(1)}, f32[8,1024]{1,0:T(8,128)}, u32[]{:S(2)}) %copy-start) | copy-done | bytes 32792
  9.5 0.0 copy-start.1
  9.6 0.7 %copy-done.1 = s32[32,1,32]{2,1,0:T(1,128)S(1)} copy-done((s32[32,1,32]{2,1,0:T(1,128)S(1)}, s32[32,1,32]{2,1,0:T(1,128)}, u32[]{:S(2)}) %copy-start.1) | copy-done | bytes 4120
  10.3 0.1 shard_map.55
  10.4 0.0 collective-permute-done.other_ref
  10.4 0.7 %shard_map.56 = f32[16,32,128]{2,1,0:T(8,128)} custom-call(f32[16,16,128]{2,1,0:T(8,128)S(1)} %get-tuple-element.10.half_ref, s32[16,8,128]{2,1,0:T(8,128)S(1)} %get-tuple-element.11.column_ref, f32[8,1024]{1,0:T(8,128)S(1)} %collective-permute-done.other_ref), custom_call_target="tpu_custom_call" | custom-call | tf_op jit(solution)/shard_map/pallas_call | solution.py:293
  11.1 10.2 %all-to-all-start = ((f32[16,32,128]{2,1,0:T(8,128)}), f32[16,32,128]{2,1,0:T(8,128)S(1)}, u32[]{:S(2)}, u32[]{:S(2)}) async-start(f32[16,32,128]{2,1,0:T(8,128)} %shard_map.56), calls=%async_computation | async-start | bytes 524288 | tf_op jit(solution)/shard_map/all_to_all | solution.py:299
  21.4 0.5 broadcast.6
  21.9 1.3 %reduce.6 = s32[32]{0:T(128)S(1)} reduce(s32[1,1,32]{2,1,0:T(1,128)} %param.7, s32[]{:T(128)} %broadcast.6), dimensions={0,1}, to_apply=%param.7.reduce_sub_computation.3 | reduce | bytes 260 | tf_op args[2]
  23.2 0.1 reshape.24
  23.3 0.1 copy.9
  23.4 0.1 broadcast_in_dim.8
  23.5 0.5 broadcast.7
  24.0 1.5 %reduce.7 = f32[8192]{0:T(1024)S(1)} reduce(f32[1,1,8192]{2,1,0:T(1,128)} %param.9, f32[]{:T(128)} %broadcast.7), dimensions={0,1}, to_apply=%param.9.reduce_sub_computation.3 | reduce | bytes 65540 | tf_op args[4]
  25.5 2.7 %copy.8 = bf16[8,2,2,4,8192]{4,0,2,1,3:T(8,128)(2,1)S(1)} copy(bf16[8,2,2,4,8192]{4,3,2,1,0:T(4,128)(2,1)} %bitcast.15) | data formatting | bytes 4194304 | tf_op jit(solution)/shard_map/reshape | solution.py:301
  28.2 1.2 %constant_dynamic-slice_fusion = s32[1,1,1]{2,1,0:T(1,128)} fusion(s32[32,1,1]{2,1,0:T(1,128)} %bitcast.14, s32[]{:T(128)S(6)} %select_n.4), kind=kLoop, calls=%fused_computation.1 | loop fusion | bytes 12 | tf_op jit(solution)/shard_map/jit(dynamic_index_in_dim)/dynamic_slice | solution.py:318
  29.4 0.1 broadcast_in_dim.9.counts_ref
  29.5 1.4 %shard_map.57 = (f32[32,1024]{1,0:T(8,128)S(1)}, f32[32,1024]{1,0:T(8,128)S(1)}, f32[8,1024]{1,0:T(8,128)S(1)}) custom-call(bf16[4,32,8192]{2,1,0:T(8,128)(2,1)S(1)} %bitcast.10, s32[32,128]{1,0:T(8,128)S(1)} %broadcast_in_dim.9.counts_ref), custom_call_target="tpu_custom_call" | custom-call | flops 2097152 | bytes 2097152 | tf_op jit(solution)/shard_map/pallas_call | solution.py:306
  30.9 0.7 %pad_add_fusion.place_ref = s32[2]{0:T(128)S(1)} fusion(s32[1]{0:T(128)} %bitcast.1, s32[1]{0:T(128)} %bitcast.core_ref), kind=kLoop, calls=%fused_computation | loop fusion | flops 2 | bytes 16 | tf_op jit(solution)/shard_map/stack | solution.py:330
  31.7 4.4 %all-to-all-done = f32[16,32,128]{2,1,0:T(8,128)S(1)} async-done(((f32[16,32,128]{2,1,0:T(8,128)}), f32[16,32,128]{2,1,0:T(8,128)S(1)}, u32[]{:S(2)}, u32[]{:S(2)}) %all-to-all-start) | async-done | bytes 262176 | tf_op jit(solution)/shard_map/all_to_all | solution.py:299
  36.1 1.9 %shard_map.58 = f32[32,9,2,128]{3,2,1,0:T(2,128)S(1)} custom-call(s32[2]{0:T(128)S(1)} %pad_add_fusion.place_ref, f32[512,128]{1,0:T(8,128)S(1)} %bitcast.12, bf16[4,32,8192]{2,1,0:T(8,128)(2,1)S(1)} %bitcast.11, s32[32,128]{1,0:T(8,128)S(1)} %broadcast_in_dim.9.counts_ref, f32[8,1024]{1,0:T(8,128)S(1)} %reshape.25.measured_ref, ...), custom_call_target="tpu_custom_call" | custom-call | flops 4194304 | bytes 2097152 | tf_op jit(solution)/shard_map/pallas_call | solution.py:319
  38.0 14.1 %all_to_all.15.parts_ref = f32[32,9,2,128]{3,2,1,0:T(2,128)S(1)} all-to-all(f32[32,9,2,128]{3,2,1,0:T(2,128)S(1)} %shard_map.58), channel_id=1, replica_groups={{10,11,8,9,14,15,12,13,2,3,0,1,6,7,4,5,26,27,24,25,30,31,28,29,18,19,16..., dimensions={0} | all-to-all | bytes 589824 | tf_op jit(solution)/shard_map/all_to_all | solution.py:339
  52.1 0.3 shard_map.59
  52.4 14.9 %all_to_all.16.parts_ref = f32[16,8,128]{2,1,0:T(8,128)S(1)} all-to-all(f32[16,8,128]{2,1,0:T(8,128)S(1)} %bitcast.13), channel_id=1, replica_groups={{288,320,352,384,416,448,480,0,32,64,96,128,160,192,224,256},{304,336,3..., dimensions={0} | all-to-all | bytes 131072 | tf_op jit(solution)/shard_map/all_to_all | solution.py:341
  67.3 0.7 %shard_map.60 = f32[8,64]{1,0:T(8,128)} custom-call(f32[16,8,128]{2,1,0:T(8,128)S(1)} %all_to_all.16.parts_ref), custom_call_target="tpu_custom_call" | custom-call | tf_op jit(solution)/shard_map/pallas_call | solution.py:342
  (1 shorter events, 0.0 us)
Async XLA Ops:
  0.0 10.4 %collective-permute-start = (f32[8,1024]{1,0:T(8,128)}, f32[8,1024]{1,0:T(8,128)S(1)}, u32[]{:S(2)}, u32[]{:S(2)}) collective-permute-start(f32[8,1024]{1,0:T(8,128)} %own_ref.1), channel_id=1, source_target_pairs={{0,16},{16,0},{32,48},{48,32},{64,80},{80,64},{96,112},{112,96},{1... | collective-permute-start | bytes 98312 | tf_op jit(solution)/shard_map/ppermute | solution.py:282
  8.8 0.8 %copy-start = (f32[8,1024]{1,0:T(8,128)S(1)}, f32[8,1024]{1,0:T(8,128)}, u32[]{:S(2)}) copy-start(f32[8,1024]{1,0:T(8,128)} %own_ref.1) | copy-start | bytes 98308
  9.5 0.7 %copy-start.1 = (s32[32,1,32]{2,1,0:T(1,128)S(1)}, s32[32,1,32]{2,1,0:T(1,128)}, u32[]{:S(2)}) copy-start(s32[32,1,32]{2,1,0:T(1,128)} %foot_ref.1) | copy-start | bytes 12292
  11.1 24.9 %all-to-all-start = ((f32[16,32,128]{2,1,0:T(8,128)}), f32[16,32,128]{2,1,0:T(8,128)S(1)}, u32[]{:S(2)}, u32[]{:S(2)}) async-start(f32[16,32,128]{2,1,0:T(8,128)} %shard_map.56), calls=%async_computation | async-start | bytes 524288 | tf_op jit(solution)/shard_map/all_to_all | solution.py:299

commit v7 on v6

--- a/solution.py
+++ b/solution.py
@@ -16,7 +16,7 @@
 N_Z = 16
 N_VIEW = 16
 PEERS = 2 * N_VIEW
-PIECE = 2
+PIECE = 1
 PIECES = HALF // PIECE
 SUB = VOXELS // N_VIEW
 FIRST_OUT = 11
@@ -214,9 +214,8 @@
     back = fold_lags(spread_ref, counts)
     for step in range(2):
         parity = step ^ odd
-        first = parity * N_VIEW
-        even = [first + (2 * tile ^ FIRST_VIEW) for tile in range(TILES)]
-        other = [first + (2 * tile + 1 ^ FIRST_VIEW) for tile in range(TILES)]
+        even = [2 * (2 * tile ^ FIRST_VIEW) + parity for tile in range(TILES)]
+        other = [2 * (2 * tile + 1 ^ FIRST_VIEW) + parity for tile in range(TILES)]
         base = (((first_owner + 1 - parity) >> 1) << 3) + (first_block & 7)
         base = jnp.full((PIECE, LANES), base, jnp.int32).astype(F32)
         part = slice(step * HALF, (step + 1) * HALF)
@@ -277,7 +276,9 @@
         [[2 * ((step * place + first) % N_Z) + c for place in range(N_Z)] for c in range(2)]
         for first, step in ((FIRST_OUT, STEP_OUT), (FIRST_BACK, STEP_BACK))
     )
-    planes = [[z * PEERS + (peer ^ FIRST_VIEW) for peer in range(PEERS)] for z in range(N_Z)]
+    planes = [
+        [(2 * z + peer % 2) * N_VIEW + (peer // 2 ^ FIRST_VIEW) for peer in range(PEERS)] for z in range(N_Z)
+    ]
 
     other = lax.ppermute(volume, "vol", swap)
     rows_scratch = pltpu.VMEM((BLK * TILES, LANES), F32)

time: 68.5 us -> 68.6 us (level)
  no operation moved by 1% of the time
where the time goes in v7:
time: 68.6 us; the launch traced here: 68 us
  blocking collectives  29.1 us (42%)
  starting transfers between devices  19 us (28%)
  local copies, waits for them, and re-layouts  6.77 us (10%)
  Pallas kernels  5.21 us (8%)
  waiting for transfers between devices  4.39 us (6%)
  other arithmetic  3.52 us (5%)
    all_to_all x1, blocking collectives, shards(): lax.all_to_all(placed.reshape(N_Z, BLK, LANES), 'vol', 0, 0, axis_index_g...  15.1 us
    all_to_all x1, blocking collectives, shards(): lax.all_to_all(parts, ('vol', 'view'), 0, 0, axis_index_groups=planes)  13.9 us
    all_to_all x1, starting transfers between devices, shards(): blocks = lax.all_to_all(sent, 'vol', 0, 0, axis_index_groups=out_chips)  10.2 us
    ppermute x1, starting transfers between devices, shards(): other = lax.ppermute(volume, 'vol', swap)  8.77 us
    all_to_all x1, waiting for transfers between devices, shards(): blocks = lax.all_to_all(sent, 'vol', 0, 0, axis_index_groups=out_chips)  4.38 us
    unnamed x2, other arithmetic  2.8 us
    reshape x1, local copies, waits for them, and re-layouts, shards(): weights = ray_weights.reshape(8, 2, 2, BAND, FOLDS * VOXELS)  2.74 us
    unnamed x6, local copies, waits for them, and re-layouts  2.5 us
  transfers between devices with their start and end apart: 2, of which 1 were waited for; matrix products, arithmetic and copies ran while one was open for 13% of the time, Pallas kernels for 2%

profile of v7, /device:TPU:1, one launch (start us, length us, event | category | flops | bytes accessed | tf_op | source)
XLA Modules:
  0.0 68.0 jit_solution(12719140622274298966)
XLA Ops:
  0.0 8.8 %collective-permute-start = (f32[8,1024]{1,0:T(8,128)}, f32[8,1024]{1,0:T(8,128)S(1)}, u32[]{:S(2)}, u32[]{:S(2)}) collective-permute-start(f32[8,1024]{1,0:T(8,128)} %own_ref.1), channel_id=1, source_target_pairs={{0,16},{16,0},{32,48},{48,32},{64,80},{80,64},{96,112},{112,96},{1... | collective-permute-start | bytes 98312 | tf_op jit(solution)/shard_map/ppermute | solution.py:283
  8.8 0.0 copy-start
  8.8 0.7 %copy-done = f32[8,1024]{1,0:T(8,128)S(1)} copy-done((f32[8,1024]{1,0:T(8,128)S(1)}, f32[8,1024]{1,0:T(8,128)}, u32[]{:S(2)}) %copy-start) | copy-done | bytes 32792
  9.5 0.0 copy-start.1
  9.6 0.7 %copy-done.1 = s32[32,1,32]{2,1,0:T(1,128)S(1)} copy-done((s32[32,1,32]{2,1,0:T(1,128)S(1)}, s32[32,1,32]{2,1,0:T(1,128)}, u32[]{:S(2)}) %copy-start.1) | copy-done | bytes 4120
  10.3 0.1 shard_map.55
  10.4 0.0 collective-permute-done.other_ref
  10.4 0.7 %shard_map.56 = f32[16,32,128]{2,1,0:T(8,128)} custom-call(f32[16,16,128]{2,1,0:T(8,128)S(1)} %get-tuple-element.10.half_ref, s32[16,8,128]{2,1,0:T(8,128)S(1)} %get-tuple-element.11.column_ref, f32[8,1024]{1,0:T(8,128)S(1)} %collective-permute-done.other_ref), custom_call_target="tpu_custom_call" | custom-call | tf_op jit(solution)/shard_map/pallas_call | solution.py:294
  11.1 10.2 %all-to-all-start = ((f32[16,32,128]{2,1,0:T(8,128)}), f32[16,32,128]{2,1,0:T(8,128)S(1)}, u32[]{:S(2)}, u32[]{:S(2)}) async-start(f32[16,32,128]{2,1,0:T(8,128)} %shard_map.56), calls=%async_computation | async-start | bytes 524288 | tf_op jit(solution)/shard_map/all_to_all | solution.py:300
  21.4 0.5 broadcast.6
  21.9 1.3 %reduce.6 = s32[32]{0:T(128)S(1)} reduce(s32[1,1,32]{2,1,0:T(1,128)} %param.7, s32[]{:T(128)} %broadcast.6), dimensions={0,1}, to_apply=%param.7.reduce_sub_computation.3 | reduce | bytes 260 | tf_op args[2]
  23.2 0.1 reshape.24
  23.3 0.1 copy.9
  23.4 0.1 broadcast_in_dim.8
  23.5 0.5 broadcast.7
  24.0 1.5 %reduce.7 = f32[8192]{0:T(1024)S(1)} reduce(f32[1,1,8192]{2,1,0:T(1,128)} %param.9, f32[]{:T(128)} %broadcast.7), dimensions={0,1}, to_apply=%param.9.reduce_sub_computation.3 | reduce | bytes 65540 | tf_op args[4]
  25.5 2.7 %copy.8 = bf16[8,2,2,4,8192]{4,0,2,1,3:T(8,128)(2,1)S(1)} copy(bf16[8,2,2,4,8192]{4,3,2,1,0:T(4,128)(2,1)} %bitcast.15) | data formatting | bytes 4194304 | tf_op jit(solution)/shard_map/reshape | solution.py:302
  28.2 1.2 %constant_dynamic-slice_fusion = s32[1,1,1]{2,1,0:T(1,128)} fusion(s32[32,1,1]{2,1,0:T(1,128)} %bitcast.14, s32[]{:T(128)S(6)} %select_n.4), kind=kLoop, calls=%fused_computation.1 | loop fusion | bytes 12 | tf_op jit(solution)/shard_map/jit(dynamic_index_in_dim)/dynamic_slice | solution.py:319
  29.4 0.1 broadcast_in_dim.9.counts_ref
  29.5 1.4 %shard_map.57 = (f32[32,1024]{1,0:T(8,128)S(1)}, f32[32,1024]{1,0:T(8,128)S(1)}, f32[8,1024]{1,0:T(8,128)S(1)}) custom-call(bf16[4,32,8192]{2,1,0:T(8,128)(2,1)S(1)} %bitcast.10, s32[32,128]{1,0:T(8,128)S(1)} %broadcast_in_dim.9.counts_ref), custom_call_target="tpu_custom_call" | custom-call | flops 2097152 | bytes 2097152 | tf_op jit(solution)/shard_map/pallas_call | solution.py:307
  30.9 0.7 %pad_add_fusion.place_ref = s32[2]{0:T(128)S(1)} fusion(s32[1]{0:T(128)} %bitcast.1, s32[1]{0:T(128)} %bitcast.core_ref), kind=kLoop, calls=%fused_computation | loop fusion | flops 2 | bytes 16 | tf_op jit(solution)/shard_map/stack | solution.py:331
  31.7 4.4 %all-to-all-done = f32[16,32,128]{2,1,0:T(8,128)S(1)} async-done(((f32[16,32,128]{2,1,0:T(8,128)}), f32[16,32,128]{2,1,0:T(8,128)S(1)}, u32[]{:S(2)}, u32[]{:S(2)}) %all-to-all-start) | async-done | bytes 262176 | tf_op jit(solution)/shard_map/all_to_all | solution.py:300
  36.1 1.9 %shard_map.58 = f32[32,17,1,128]{3,2,1,0:T(1,128)S(1)} custom-call(s32[2]{0:T(128)S(1)} %pad_add_fusion.place_ref, f32[512,128]{1,0:T(8,128)S(1)} %bitcast.12, bf16[4,32,8192]{2,1,0:T(8,128)(2,1)S(1)} %bitcast.11, s32[32,128]{1,0:T(8,128)S(1)} %broadcast_in_dim.9.counts_ref, f32[8,1024]{1,0:T(8,128)S(1)} %reshape.25.measured_ref, ...), custom_call_target="tpu_custom_call" | custom-call | flops 4194304 | bytes 2097152 | tf_op jit(solution)/shard_map/pallas_call | solution.py:320
  38.0 13.9 %all_to_all.15.parts_ref = f32[32,17,1,128]{3,2,1,0:T(1,128)S(1)} all-to-all(f32[32,17,1,128]{3,2,1,0:T(1,128)S(1)} %shard_map.58), channel_id=1, replica_groups={{10,26,11,27,8,24,9,25,14,30,15,31,12,28,13,29,2,18,3,19,0,16,1,17,6,22..., dimensions={0} | all-to-all | bytes 557056 | tf_op jit(solution)/shard_map/all_to_all | solution.py:340
  51.9 0.3 shard_map.59
  52.2 15.1 %all_to_all.16.parts_ref = f32[16,8,128]{2,1,0:T(8,128)S(1)} all-to-all(f32[16,8,128]{2,1,0:T(8,128)S(1)} %bitcast.13), channel_id=1, replica_groups={{288,320,352,384,416,448,480,0,32,64,96,128,160,192,224,256},{304,336,3..., dimensions={0} | all-to-all | bytes 131072 | tf_op jit(solution)/shard_map/all_to_all | solution.py:342
  67.4 0.7 %shard_map.60 = f32[8,64]{1,0:T(8,128)} custom-call(f32[16,8,128]{2,1,0:T(8,128)S(1)} %all_to_all.16.parts_ref), custom_call_target="tpu_custom_call" | custom-call | tf_op jit(solution)/shard_map/pallas_call | solution.py:343
  (1 shorter events, 0.0 us)
Async XLA Ops:
  0.0 10.4 %collective-permute-start = (f32[8,1024]{1,0:T(8,128)}, f32[8,1024]{1,0:T(8,128)S(1)}, u32[]{:S(2)}, u32[]{:S(2)}) collective-permute-start(f32[8,1024]{1,0:T(8,128)} %own_ref.1), channel_id=1, source_target_pairs={{0,16},{16,0},{32,48},{48,32},{64,80},{80,64},{96,112},{112,96},{1... | collective-permute-start | bytes 98312 | tf_op jit(solution)/shard_map/ppermute | solution.py:283
  8.8 0.8 %copy-start = (f32[8,1024]{1,0:T(8,128)S(1)}, f32[8,1024]{1,0:T(8,128)}, u32[]{:S(2)}) copy-start(f32[8,1024]{1,0:T(8,128)} %own_ref.1) | copy-start | bytes 98308
  9.5 0.7 %copy-start.1 = (s32[32,1,32]{2,1,0:T(1,128)S(1)}, s32[32,1,32]{2,1,0:T(1,128)}, u32[]{:S(2)}) copy-start(s32[32,1,32]{2,1,0:T(1,128)} %foot_ref.1) | copy-start | bytes 12292
  11.1 24.9 %all-to-all-start = ((f32[16,32,128]{2,1,0:T(8,128)}), f32[16,32,128]{2,1,0:T(8,128)S(1)}, u32[]{:S(2)}, u32[]{:S(2)}) async-start(f32[16,32,128]{2,1,0:T(8,128)} %shard_map.56), calls=%async_computation | async-start | bytes 524288 | tf_op jit(solution)/shard_map/all_to_all | solution.py:300

commit v8 on v6

--- a/solution.py
+++ b/solution.py
@@ -21,7 +21,7 @@
 SUB = VOXELS // N_VIEW
 FIRST_OUT = 11
 FIRST_BACK = 9
-FIRST_VIEW = 10
+FIRST_VIEW = 15
 STEP_OUT = 9
 STEP_BACK = 1
 

time: 68.5 us -> 70.1 us (1.023)
  blocking collectives: 29 us -> 30.6 us
    all_to_all x1, blocking collectives: 14.1 us -> 15.5 us  [shards(): lax.all_to_all(parts, ('vol', 'view'), 0, 0, axis_index_groups=planes)]
where the time goes in v8:
time: 70.1 us; the launch traced here: 69.6 us
  blocking collectives  30.6 us (44%)
  starting transfers between devices  19 us (27%)
  local copies, waits for them, and re-layouts  6.77 us (10%)
  Pallas kernels  5.19 us (7%)
  waiting for transfers between devices  4.39 us (6%)
  other arithmetic  3.52 us (5%)
    all_to_all x1, blocking collectives, shards(): lax.all_to_all(parts, ('vol', 'view'), 0, 0, axis_index_groups=planes)  15.5 us
    all_to_all x1, blocking collectives, shards(): lax.all_to_all(placed.reshape(N_Z, BLK, LANES), 'vol', 0, 0, axis_index_g...  15.1 us
    all_to_all x1, starting transfers between devices, shards(): blocks = lax.all_to_all(sent, 'vol', 0, 0, axis_index_groups=out_chips)  10.2 us
    ppermute x1, starting transfers between devices, shards(): other = lax.ppermute(volume, 'vol', swap)  8.77 us
    all_to_all x1, waiting for transfers between devices, shards(): blocks = lax.all_to_all(sent, 'vol', 0, 0, axis_index_groups=out_chips)  4.38 us
    unnamed x2, other arithmetic  2.8 us
    reshape x1, local copies, waits for them, and re-layouts, shards(): weights = ray_weights.reshape(8, 2, 2, BAND, FOLDS * VOXELS)  2.74 us
    unnamed x6, local copies, waits for them, and re-layouts  2.5 us
  transfers between devices with their start and end apart: 2, of which 1 were waited for; matrix products, arithmetic and copies ran while one was open for 13% of the time, Pallas kernels for 2%

profile of v8, /device:TPU:1, one launch (start us, length us, event | category | flops | bytes accessed | tf_op | source)
XLA Modules:
  0.0 69.6 jit_solution(266030142698828723)
XLA Ops:
  0.0 8.8 %collective-permute-start = (f32[8,1024]{1,0:T(8,128)}, f32[8,1024]{1,0:T(8,128)S(1)}, u32[]{:S(2)}, u32[]{:S(2)}) collective-permute-start(f32[8,1024]{1,0:T(8,128)} %own_ref.1), channel_id=1, source_target_pairs={{0,16},{16,0},{32,48},{48,32},{64,80},{80,64},{96,112},{112,96},{1... | collective-permute-start | bytes 98312 | tf_op jit(solution)/shard_map/ppermute | solution.py:282
  8.8 0.0 copy-start
  8.8 0.7 %copy-done = f32[8,1024]{1,0:T(8,128)S(1)} copy-done((f32[8,1024]{1,0:T(8,128)S(1)}, f32[8,1024]{1,0:T(8,128)}, u32[]{:S(2)}) %copy-start) | copy-done | bytes 32792
  9.5 0.0 copy-start.1
  9.6 0.7 %copy-done.1 = s32[32,1,32]{2,1,0:T(1,128)S(1)} copy-done((s32[32,1,32]{2,1,0:T(1,128)S(1)}, s32[32,1,32]{2,1,0:T(1,128)}, u32[]{:S(2)}) %copy-start.1) | copy-done | bytes 4120
  10.3 0.1 shard_map.55
  10.4 0.0 collective-permute-done.other_ref
  10.4 0.7 %shard_map.56 = f32[16,32,128]{2,1,0:T(8,128)} custom-call(f32[16,16,128]{2,1,0:T(8,128)S(1)} %get-tuple-element.10.half_ref, s32[16,8,128]{2,1,0:T(8,128)S(1)} %get-tuple-element.11.column_ref, f32[8,1024]{1,0:T(8,128)S(1)} %collective-permute-done.other_ref), custom_call_target="tpu_custom_call" | custom-call | tf_op jit(solution)/shard_map/pallas_call | solution.py:293
  11.1 10.2 %all-to-all-start = ((f32[16,32,128]{2,1,0:T(8,128)}), f32[16,32,128]{2,1,0:T(8,128)S(1)}, u32[]{:S(2)}, u32[]{:S(2)}) async-start(f32[16,32,128]{2,1,0:T(8,128)} %shard_map.56), calls=%async_computation | async-start | bytes 524288 | tf_op jit(solution)/shard_map/all_to_all | solution.py:299
  21.4 0.5 broadcast.6
  21.9 1.3 %reduce.6 = s32[32]{0:T(128)S(1)} reduce(s32[1,1,32]{2,1,0:T(1,128)} %param.7, s32[]{:T(128)} %broadcast.6), dimensions={0,1}, to_apply=%param.7.reduce_sub_computation.3 | reduce | bytes 260 | tf_op args[2]
  23.2 0.1 reshape.24
  23.3 0.1 copy.9
  23.4 0.1 broadcast_in_dim.8
  23.5 0.5 broadcast.7
  24.0 1.5 %reduce.7 = f32[8192]{0:T(1024)S(1)} reduce(f32[1,1,8192]{2,1,0:T(1,128)} %param.9, f32[]{:T(128)} %broadcast.7), dimensions={0,1}, to_apply=%param.9.reduce_sub_computation.3 | reduce | bytes 65540 | tf_op args[4]
  25.5 2.7 %copy.8 = bf16[8,2,2,4,8192]{4,0,2,1,3:T(8,128)(2,1)S(1)} copy(bf16[8,2,2,4,8192]{4,3,2,1,0:T(4,128)(2,1)} %bitcast.15) | data formatting | bytes 4194304 | tf_op jit(solution)/shard_map/reshape | solution.py:301
  28.2 1.2 %constant_dynamic-slice_fusion = s32[1,1,1]{2,1,0:T(1,128)} fusion(s32[32,1,1]{2,1,0:T(1,128)} %bitcast.14, s32[]{:T(128)S(6)} %select_n.4), kind=kLoop, calls=%fused_computation.1 | loop fusion | bytes 12 | tf_op jit(solution)/shard_map/jit(dynamic_index_in_dim)/dynamic_slice | solution.py:318
  29.4 0.1 broadcast_in_dim.9.counts_ref
  29.5 1.4 %shard_map.57 = (f32[32,1024]{1,0:T(8,128)S(1)}, f32[32,1024]{1,0:T(8,128)S(1)}, f32[8,1024]{1,0:T(8,128)S(1)}) custom-call(bf16[4,32,8192]{2,1,0:T(8,128)(2,1)S(1)} %bitcast.10, s32[32,128]{1,0:T(8,128)S(1)} %broadcast_in_dim.9.counts_ref), custom_call_target="tpu_custom_call" | custom-call | flops 2097152 | bytes 2097152 | tf_op jit(solution)/shard_map/pallas_call | solution.py:306
  30.9 0.7 %pad_add_fusion.place_ref = s32[2]{0:T(128)S(1)} fusion(s32[1]{0:T(128)} %bitcast.1, s32[1]{0:T(128)} %bitcast.core_ref), kind=kLoop, calls=%fused_computation | loop fusion | flops 2 | bytes 16 | tf_op jit(solution)/shard_map/stack | solution.py:330
  31.7 4.4 %all-to-all-done = f32[16,32,128]{2,1,0:T(8,128)S(1)} async-done(((f32[16,32,128]{2,1,0:T(8,128)}), f32[16,32,128]{2,1,0:T(8,128)S(1)}, u32[]{:S(2)}, u32[]{:S(2)}) %all-to-all-start) | async-done | bytes 262176 | tf_op jit(solution)/shard_map/all_to_all | solution.py:299
  36.1 1.9 %shard_map.58 = f32[32,9,2,128]{3,2,1,0:T(2,128)S(1)} custom-call(s32[2]{0:T(128)S(1)} %pad_add_fusion.place_ref, f32[512,128]{1,0:T(8,128)S(1)} %bitcast.12, bf16[4,32,8192]{2,1,0:T(8,128)(2,1)S(1)} %bitcast.11, s32[32,128]{1,0:T(8,128)S(1)} %broadcast_in_dim.9.counts_ref, f32[8,1024]{1,0:T(8,128)S(1)} %reshape.25.measured_ref, ...), custom_call_target="tpu_custom_call" | custom-call | flops 4194304 | bytes 2097152 | tf_op jit(solution)/shard_map/pallas_call | solution.py:319
  38.0 15.5 %all_to_all.15.parts_ref = f32[32,9,2,128]{3,2,1,0:T(2,128)S(1)} all-to-all(f32[32,9,2,128]{3,2,1,0:T(2,128)S(1)} %shard_map.58), channel_id=1, replica_groups={{15,14,13,12,11,10,9,8,7,6,5,4,3,2,1,0,31,30,29,28,27,26,25,24,23,22,21..., dimensions={0} | all-to-all | bytes 589824 | tf_op jit(solution)/shard_map/all_to_all | solution.py:339
  53.5 0.3 shard_map.59
  53.8 15.1 %all_to_all.16.parts_ref = f32[16,8,128]{2,1,0:T(8,128)S(1)} all-to-all(f32[16,8,128]{2,1,0:T(8,128)S(1)} %bitcast.13), channel_id=1, replica_groups={{288,320,352,384,416,448,480,0,32,64,96,128,160,192,224,256},{304,336,3..., dimensions={0} | all-to-all | bytes 131072 | tf_op jit(solution)/shard_map/all_to_all | solution.py:341
  68.9 0.7 shard_map.60
  (1 shorter events, 0.0 us)
Async XLA Ops:
  0.0 10.4 %collective-permute-start = (f32[8,1024]{1,0:T(8,128)}, f32[8,1024]{1,0:T(8,128)S(1)}, u32[]{:S(2)}, u32[]{:S(2)}) collective-permute-start(f32[8,1024]{1,0:T(8,128)} %own_ref.1), channel_id=1, source_target_pairs={{0,16},{16,0},{32,48},{48,32},{64,80},{80,64},{96,112},{112,96},{1... | collective-permute-start | bytes 98312 | tf_op jit(solution)/shard_map/ppermute | solution.py:282
  8.8 0.8 %copy-start = (f32[8,1024]{1,0:T(8,128)S(1)}, f32[8,1024]{1,0:T(8,128)}, u32[]{:S(2)}) copy-start(f32[8,1024]{1,0:T(8,128)} %own_ref.1) | copy-start | bytes 98308
  9.5 0.7 %copy-start.1 = (s32[32,1,32]{2,1,0:T(1,128)S(1)}, s32[32,1,32]{2,1,0:T(1,128)}, u32[]{:S(2)}) copy-start(s32[32,1,32]{2,1,0:T(1,128)} %foot_ref.1) | copy-start | bytes 12292
  11.1 24.9 %all-to-all-start = ((f32[16,32,128]{2,1,0:T(8,128)}), f32[16,32,128]{2,1,0:T(8,128)S(1)}, u32[]{:S(2)}, u32[]{:S(2)}) async-start(f32[16,32,128]{2,1,0:T(8,128)} %shard_map.56), calls=%async_computation | async-start | bytes 524288 | tf_op jit(solution)/shard_map/all_to_all | solution.py:299
